TPU v7x, 32 devices: a whole 2x2x4 slice. The times are simulated.
32 devices in a mesh: req: 2 (over x), exp: 16 (over z, y, core).
Axes of the slice: x: 2, y: 2, z: 4, core: 2. Of those that a mesh axis runs over, the one named last changes fastest.
Arguments:
- attn_out: bfloat16 [4096, 2048], P(('req', 'exp')), may hold values from -6 to 6
- residual: bfloat16 [4096, 2048], P(('req', 'exp')), may hold values from -6 to 6
- out_weight: bfloat16 [2048, 2048], P('exp'), may hold values from -0.125 to 0.125
- norm_gain: float32 [2048], replicated, may hold values from 0.25 to 1.75
- expert_ids: int32 [4096, 6], P(('req', 'exp')), may hold values from 0 to 15, all different within a row; in each aligned block of 128 rows (0 to 127, 128 to 255, ...) at most 72 rows name the same one
- gate_weights: float32 [4096, 6], P(('req', 'exp')), may hold values from 0.05 to 0.5
- expert_gate: bfloat16 [16, 2048, 1408], P('exp'), may hold values from -0.125 to 0.125
- expert_up: bfloat16 [16, 2048, 1408], P('exp'), may hold values from -0.125 to 0.125
- expert_down: bfloat16 [16, 1408, 2048], P('exp'), may hold values from -0.15625 to 0.15625
- shared_gate: bfloat16 [2048, 1408], P(None, 'req'), may hold values from -0.125 to 0.125
- shared_up: bfloat16 [2048, 1408], P(None, 'req'), may hold values from -0.125 to 0.125
- shared_down: bfloat16 [2048, 1408], P(None, 'req'), may hold values from -0.15625 to 0.15625
Outputs:
- mixed: bfloat16 [4096, 2048], P(('req', 'exp'))
Inputs may be any that keep to these rules, and one draw needn't show every extreme that they name: `expert_ids`: within the rows of one device no expert is named by more than 72 rows, and each row names 6 different experts.
All inputs are finite; a program needn't handle non-finite values.
Results may differ from a plain program's by a relative error of at most 0.012.
Values may be sent and summed in bfloat16 or wider, within the bound.
No kernel may reach another device: no remote copies, remote signals or barrier semaphores. Data moves between devices by JAX's collectives and lax.ppermute only.
A program may use at most 192 MiB of HBM per device.

v0:
```python
import functools

import jax
import jax.numpy as jnp
from jax import lax
from jax.experimental import pallas as pl
from jax.experimental.pallas import tpu as pltpu
from jax.sharding import PartitionSpec as P

F32 = jnp.float32
BF16 = jnp.bfloat16
VMEM_BYTES = 12 * 1024 * 1024
TILE = 512
TABLE_ROWS = 16


def ring_order(chips):
    slow = 4
    fast = chips // slow
    order = [a * fast for a in range(slow)]
    for turn, a in enumerate(reversed(range(slow))):
        inner = range(1, fast) if turn % 2 == 0 else range(fast - 1, 0, -1)
        order += [a * fast + b for b in inner]
    return order


def mm(a, b):
    return jnp.dot(a, b, preferred_element_type=F32)


def vmem():
    return pl.BlockSpec(memory_space=pltpu.VMEM)


def smem():
    return pl.BlockSpec(memory_space=pltpu.SMEM)


def hbm():
    return pl.BlockSpec(memory_space=pl.ANY)


def params():
    return pltpu.CompilerParams(vmem_limit_bytes=VMEM_BYTES)


def prepare_kernel(part, where_ref, ids_hbm, factors_hbm, weight_hbm, own_ref, sent_ref, ids_ref, factors_ref, sems):
    wrows, width = weight_hbm.shape
    topk, rows = ids_ref.shape
    core, request = where_ref[1], where_ref[2]
    small = [
        pltpu.make_async_copy(ids_hbm, ids_ref, sems.at[2]),
        pltpu.make_async_copy(factors_hbm, factors_ref, sems.at[3]),
    ]
    large = []
    for i, (ref, which) in enumerate(((own_ref, core), (sent_ref, 1 - core))):
        start = pl.multiple_of(which * (width // 2) + request * part, 128)
        large.append(pltpu.make_async_copy(weight_hbm.at[:, pl.ds(start, part)], ref.at[:wrows], sems.at[i]))
    for copy in small + large:
        copy.start()
    for copy in small:
        copy.wait()
    per_row = part // rows
    factors = factors_ref[...]
    big = factors.astype(BF16).astype(F32)
    middle = (factors - big).astype(BF16).astype(F32)
    named = (ids_ref[...].astype(F32), big, middle, factors - big - middle)
    items = [kind[k : k + 1] for kind in named for k in range(topk)]
    items += [jnp.zeros((1, rows), F32)] * (-len(items) % per_row)
    lines = [jnp.concatenate(items[i : i + per_row], axis=1) for i in range(0, len(items), per_row)]
    lines.append(jnp.zeros((TABLE_ROWS - len(lines), part), F32))
    table = jnp.concatenate(lines, axis=0).astype(BF16)
    own_ref[wrows:] = table
    sent_ref[wrows:] = table
    for copy in large:
        copy.wait()


def prepare(part, where, ids, factors, weight):
    shape = jax.ShapeDtypeStruct((weight.shape[0] + TABLE_ROWS, part), BF16)
    arrays = [pltpu.with_memory_space_constraint(x, pltpu.HBM) for x in (ids, factors, weight)]
    return pl.pallas_call(
        functools.partial(prepare_kernel, part),
        out_shape=[shape] * 2,
        in_specs=[smem()] + [hbm()] * 3,
        out_specs=[vmem()] * 2,
        scratch_shapes=[
            pltpu.VMEM(ids.shape, ids.dtype),
            pltpu.VMEM(factors.shape, factors.dtype),
            pltpu.SemaphoreType.DMA((4,)),
        ],
        compiler_params=params(),
        cost_estimate=pl.CostEstimate(flops=0, bytes_accessed=2 * weight.size, transcendentals=0),
        name="prepare",
    )(where, *arrays)


def small_call(kernel, name, shapes, operands, moved):
    return pl.pallas_call(
        kernel,
        out_shape=shapes,
        in_specs=[smem()] + [vmem()] * (len(operands) - 1),
        out_specs=[vmem()] * len(shapes),
        compiler_params=params(),
        cost_estimate=pl.CostEstimate(flops=0, bytes_accessed=moved, transcendentals=0),
        name=name,
    )(*operands)


def join_kernel(where_ref, mine_ref, other_ref, out_ref):
    rows = mine_ref.shape[0]
    core = where_ref[1]
    out_ref[pl.ds(pl.multiple_of(core * rows, 16), rows)] = mine_ref[...]
    out_ref[pl.ds(pl.multiple_of((1 - core) * rows, 16), rows)] = other_ref[...]


def join(where, mine, other):
    shape = jax.ShapeDtypeStruct((2 * mine.shape[0], mine.shape[1]), mine.dtype)
    return small_call(join_kernel, "join", [shape], [where, mine, other], 8 * mine.size)[0]


def pack_kernel(count, part, where_ref, attn_hbm, residual_hbm, *refs):
    width = attn_hbm.shape[1]
    outs, sems = refs[:-1], refs[-1]
    copies = []
    for shift, out_ref in enumerate(outs):
        moves = [(attn_hbm, out_ref.at[:, :width])]
        request = lax.rem(where_ref[2] + shift, count)
        for core in range(2):
            start = pl.multiple_of(core * (width // 2) + request * part, 128)
            target = out_ref.at[:, width + core * part : width + (core + 1) * part]
            moves.append((residual_hbm.at[:, pl.ds(start, part)], target))
        for i, (source, target) in enumerate(moves):
            copies.append(pltpu.make_async_copy(source, target, sems.at[3 * shift + i]))
    for copy in copies:
        copy.start()
    for copy in copies:
        copy.wait()


def pack(count, part, where, attn, residual):
    rows, width = attn.shape
    arrays = [pltpu.with_memory_space_constraint(x, pltpu.HBM) for x in (attn, residual)]
    return pl.pallas_call(
        functools.partial(pack_kernel, count, part),
        out_shape=[jax.ShapeDtypeStruct((rows, width + 2 * part), BF16)] * count,
        in_specs=[smem(), hbm(), hbm()],
        out_specs=[vmem()] * count,
        scratch_shapes=[pltpu.SemaphoreType.DMA((3 * count,))],
        compiler_params=params(),
        cost_estimate=pl.CostEstimate(flops=0, bytes_accessed=4 * attn.size * count, transcendentals=0),
        name="pack",
    )(where, *arrays)


def beside_kernel(where_ref, *refs):
    part = refs[0].shape[1]
    for i, ref in enumerate(refs[:-1]):
        refs[-1][:, i * part : (i + 1) * part] = ref[...]


def beside(where, pieces):
    rows, part = pieces[0].shape
    shape = jax.ShapeDtypeStruct((rows, len(pieces) * part), BF16)
    return small_call(beside_kernel, "beside", [shape], [where] + pieces, 4 * rows * part * len(pieces))[0]


def weave_kernel(count, where_ref, *refs):
    out_ref = refs[-1]
    part = out_ref.shape[1] // (2 * count)
    place = 0
    for ref in refs[:-1]:
        for at in range(ref.shape[1] // (2 * part)):
            request = lax.rem(where_ref[2] + place, count)
            place += 1
            for swap in range(2):
                core = where_ref[1] if swap == 0 else 1 - where_ref[1]
                start = pl.multiple_of(core * (count * part) + request * part, 128)
                out_ref[:, pl.ds(start, part)] = ref[:, (2 * at + swap) * part : (2 * at + swap + 1) * part]


def weave(count, where, pieces):
    rows = pieces[0].shape[0]
    width = sum(p.shape[1] for p in pieces)
    shape = jax.ShapeDtypeStruct((rows, width), BF16)
    return small_call(functools.partial(weave_kernel, count), "weave", [shape], [where] + pieces, 4 * rows * width)[0]


def proj_kernel(wrows, part, blocks, visits, final, where_ref, ring_ref, *refs):
    total = None
    rows_refs = refs[:visits]
    width = rows_refs[0].shape[1] - 2 * part
    at = visits
    chips = ring_ref.shape[0] // 2
    position = ring_ref[where_ref[0] // 2]
    for offset, pieces in blocks:
        chip = ring_ref[chips + lax.rem(position + offset + chips, chips)]
        start = pl.multiple_of(chip * 2 * wrows, 128)
        columns = jnp.concatenate([r[:, pl.ds(start, 2 * wrows)] for r in rows_refs], axis=0)
        step = wrows + TABLE_ROWS
        if pieces == 1:
            parts = [refs[at][i * step : i * step + wrows] for i in range(2)]
        else:
            parts = [refs[at + i][:wrows] for i in range(2)]
        at += pieces
        term = mm(columns, jnp.concatenate(parts, axis=0))
        total = term if total is None else total + term
    if final:
        total = total + refs[at][...]
        start = pl.multiple_of(width + where_ref[1] * part, 128)
        rows = rows_refs[0].shape[0]
        for i, out_ref in enumerate(refs[at + 1 :]):
            residual = rows_refs[i][:, pl.ds(start, part)].astype(F32)
            out_ref[...] = (residual + total[i * rows : (i + 1) * rows]).astype(BF16)
    else:
        refs[at][...] = total


def proj(wrows, blocks, where, ring, visits, weights, acc=None):
    final = acc is not None
    rows, part = visits[0].shape[0], weights[0].shape[1]
    operands = [where, ring] + visits + weights + ([acc] if final else [])
    count = len(visits)
    if final:
        outs = [jax.ShapeDtypeStruct((rows, part), BF16)] * count
    else:
        outs = [jax.ShapeDtypeStruct((rows * count, part), F32)]
    return pl.pallas_call(
        functools.partial(proj_kernel, wrows, part, blocks, count, final),
        out_shape=outs,
        in_specs=[smem()] * 2 + [vmem()] * (len(operands) - 2),
        out_specs=[vmem()] * len(outs),
        compiler_params=params(),
        cost_estimate=pl.CostEstimate(
            flops=8 * rows * count * part * wrows * len(blocks),
            bytes_accessed=4 * part * wrows * len(blocks) + 8 * rows * count * part,
            transcendentals=0,
        ),
        name="proj_final" if final else "proj_part",
    )(*operands)


def tables_kernel(wrows, slots, topk, rows, pieces, where_ref, *refs):
    pick_ref, put_ref, factor_ref = refs[-3:]
    both = 2 * rows
    expert_id = where_ref[0].astype(F32)
    first_core = where_ref[1] == 0
    row_of = lax.broadcasted_iota(jnp.int32, (both, both), 0)
    row_at = lax.broadcasted_iota(jnp.int32, (both, both), 1)
    slot_of = lax.broadcasted_iota(jnp.int32, (slots, both), 0).astype(F32)
    slot_at = lax.broadcasted_iota(jnp.int32, (both, slots), 1).astype(F32)
    step = wrows + TABLE_ROWS
    at = 0
    for block in range(pick_ref.shape[0]):
        if pieces[block] == 1:
            named = [refs[at][i * step + wrows : (i + 1) * step] for i in range(2)]
        else:
            named = [refs[at + i][wrows:] for i in range(2)]
        at += pieces[block]
        named = [n.astype(F32) for n in named]
        ordered = [jnp.where(first_core, named[0], named[1]), jnp.where(first_core, named[1], named[0])]
        per_row = named[0].shape[1] // rows
        selected, factor = [], []
        for n in ordered:
            item = [n[i // per_row : i // per_row + 1, (i % per_row) * rows : (i % per_row + 1) * rows] for i in range(4 * topk)]
            hits = [item[k] == expert_id for k in range(topk)]
            values = [item[topk + k] + item[2 * topk + k] + item[3 * topk + k] for k in range(topk)]
            selected.append(sum(h.astype(F32) for h in hits))
            factor.append(sum(jnp.where(h, v, 0.0) for h, v in zip(hits, values)))
        selected = jnp.concatenate(selected, axis=1)
        factor = jnp.concatenate(factor, axis=1)
        spread = jnp.broadcast_to(selected, (both, both))
        before = jnp.sum(jnp.where(row_at < row_of, spread, 0.0), axis=1, keepdims=True)
        selected_down = jnp.sum(jnp.where(row_at == row_of, spread, 0.0), axis=1, keepdims=True)
        slot_down = jnp.where(selected_down > 0.0, before, -1.0)
        put_ref[block] = (slot_at == slot_down).astype(F32).astype(BF16)
        slot = jnp.sum(jnp.where(row_at == row_of, jnp.broadcast_to(slot_down, (both, both)), 0.0), axis=0, keepdims=True)
        taken = slot_of == slot
        pick_ref[block] = taken.astype(F32).astype(BF16)
        factor_ref[block] = jnp.sum(jnp.where(taken, factor, 0.0), axis=1, keepdims=True)


def tables(wrows, slots, topk, rows, where, pieces, blocks):
    chips = len(pieces)
    both = 2 * rows
    return pl.pallas_call(
        functools.partial(tables_kernel, wrows, slots, topk, rows, pieces),
        out_shape=[
            jax.ShapeDtypeStruct((chips, slots, both), BF16),
            jax.ShapeDtypeStruct((chips, both, slots), BF16),
            jax.ShapeDtypeStruct((chips, slots, 1), F32),
        ],
        in_specs=[smem()] + [vmem()] * len(blocks),
        out_specs=[vmem()] * 3,
        compiler_params=params(),
        cost_estimate=pl.CostEstimate(flops=0, bytes_accessed=8 * chips * slots * both, transcendentals=0),
        name="tables",
    )(where, *blocks)


def expert_kernel(first, blocks, pieces, gain_ref, pick_ref, put_ref, factor_ref, gate_ref, up_ref, down_ref, *refs):
    slots, rows = pick_ref.shape[1:]
    own = rows // 2
    width = gain_ref.shape[1]
    hidden_units = gate_ref.shape[1]
    inputs = refs[: blocks * pieces]
    mine = refs[blocks * pieces : blocks * pieces + blocks]
    theirs, normed, hidden = refs[-3:]

    for b in range(blocks):
        block = jnp.concatenate([inputs[b * pieces + i][...] for i in range(pieces)], axis=0)
        taken = mm(pick_ref[first + b], block)
        scale = lax.rsqrt(jnp.sum(taken * taken, axis=1, keepdims=True) * (1.0 / width) + 1e-06)
        normed[b * slots : (b + 1) * slots, :] = (taken * scale * gain_ref[...]).astype(BF16)

    for start in range(0, hidden_units, TILE):
        columns = slice(start, min(start + TILE, hidden_units))
        gate_part = mm(normed[...], gate_ref[:, columns])
        up_part = mm(normed[...], up_ref[:, columns])
        hidden[:, columns] = (jax.nn.silu(gate_part) * up_part).astype(BF16)

    for start in range(0, width, TILE):
        columns = slice(start, start + TILE)
        result = mm(hidden[...], down_ref[:, columns])
        for b in range(blocks):
            weighted = (result[b * slots : (b + 1) * slots] * factor_ref[first + b]).astype(BF16)
            placed = mm(put_ref[first + b], weighted).astype(BF16)
            mine[b][:, columns] = placed[:own]
            theirs[b * own : (b + 1) * own, columns] = placed[own:]


def expert(first, blocks, tabs, gain, weights, inputs):
    slots, rows = tabs[0].shape[1:]
    width, hidden_units = weights[0].shape
    own = rows // 2
    m = blocks * slots
    weights = [pltpu.with_memory_space_constraint(w, pltpu.VMEM) for w in weights]
    out = pl.pallas_call(
        functools.partial(expert_kernel, first, blocks, len(inputs) // blocks),
        out_shape=[jax.ShapeDtypeStruct((own, width), BF16)] * blocks
        + [jax.ShapeDtypeStruct((blocks * own, width), BF16)],
        in_specs=[vmem()] * (7 + len(inputs)),
        out_specs=[vmem()] * (blocks + 1),
        scratch_shapes=[
            pltpu.VMEM((m, width), BF16),
            pltpu.VMEM((m, hidden_units), BF16),
        ],
        compiler_params=params(),
        cost_estimate=pl.CostEstimate(
            flops=12 * m * width * hidden_units,
            bytes_accessed=8 * blocks * rows * width,
            transcendentals=m * hidden_units,
        ),
        name="expert",
    )(gain, *tabs, *weights, *inputs)
    return out[:-1], out[-1]


def shared_kernel(count, gain_ref, gate_hbm, up_hbm, down_hbm, *refs):
    inputs, outs = refs[:count], refs[count : 2 * count]
    gate_ref, up_ref, down_ref, normed, hidden, sems = refs[2 * count :]
    units, width = gate_ref.shape
    rows = inputs[0].shape[0]
    tiles = [(start, min(256, units - start)) for start in range(0, units, 256)]
    copies = []
    for i, (start, size) in enumerate(tiles):
        span = pl.ds(start, size)
        for j, (source, target) in enumerate(((gate_hbm, gate_ref), (up_hbm, up_ref))):
            copies.append(pltpu.make_async_copy(source.at[span], target.at[span], sems.at[2 * i + j]))
    copies.append(pltpu.make_async_copy(down_hbm, down_ref, sems.at[2 * len(tiles)]))
    for copy in copies:
        copy.start()
    for i, ref in enumerate(inputs):
        x = ref[...].astype(F32)
        scale = lax.rsqrt(jnp.sum(x * x, axis=1, keepdims=True) * (1.0 / width) + 1e-06)
        normed[i * rows : (i + 1) * rows] = (x * scale * gain_ref[...]).astype(BF16)
    across = (((1,), (1,)), ((), ()))
    for i, (start, size) in enumerate(tiles):
        span = slice(start, start + size)
        copies[2 * i].wait()
        copies[2 * i + 1].wait()
        gate_part = lax.dot_general(normed[...], gate_ref[span], across, preferred_element_type=F32)
        up_part = lax.dot_general(normed[...], up_ref[span], across, preferred_element_type=F32)
        hidden[:, span] = (jax.nn.silu(gate_part) * up_part).astype(BF16)
    copies[-1].wait()
    for start in range(0, width, TILE):
        span = slice(start, start + TILE)
        result = mm(hidden[...], down_ref[:, span])
        for i, ref in enumerate(outs):
            ref[:, span] = result[i * rows : (i + 1) * rows].astype(ref.dtype)


def shared_expert(gain, weights, inputs):
    count = len(inputs)
    rows, width = inputs[0].shape
    units = weights[0].shape[0]
    weights = [pltpu.with_memory_space_constraint(w, pltpu.HBM) for w in weights]
    shapes = [jax.ShapeDtypeStruct((rows, width), F32)] + [jax.ShapeDtypeStruct((rows, width), BF16)] * (count - 1)
    return pl.pallas_call(
        functools.partial(shared_kernel, count),
        out_shape=shapes,
        in_specs=[vmem()] + [hbm()] * 3 + [vmem()] * count,
        out_specs=[vmem()] * count,
        scratch_shapes=[pltpu.VMEM((units, width), BF16)] * 3
        + [
            pltpu.VMEM((count * rows, width), BF16),
            pltpu.VMEM((count * rows, units), BF16),
            pltpu.SemaphoreType.DMA((2 * -(-units // 256) + 1,)),
        ],
        compiler_params=pltpu.CompilerParams(vmem_limit_bytes=24 * 1024 * 1024),
        cost_estimate=pl.CostEstimate(
            flops=12 * count * rows * width * units,
            bytes_accessed=6 * units * width + 4 * count * rows * width,
            transcendentals=count * rows * units,
        ),
        name="shared",
    )(gain, *weights, *inputs)


def base_kernel(*refs):
    total = refs[0][...]
    for ref in refs[1:-1]:
        total = total + ref[...].astype(F32)
    refs[-1][...] = total


def final_kernel(chunks, base_ref, *refs):
    out_ref = refs[-1]
    rows = refs[0].shape[0]
    for chunk in range(chunks):
        span = slice(chunk * rows, (chunk + 1) * rows)
        total = base_ref[span] + refs[chunk][...].astype(F32) + refs[chunks + chunk][...].astype(F32)
        out_ref[span] = total.astype(BF16)


def plain_call(kernel, name, shape, operands):
    return pl.pallas_call(
        kernel,
        out_shape=shape,
        in_specs=[vmem()] * len(operands),
        out_specs=vmem(),
        compiler_params=params(),
        cost_estimate=pl.CostEstimate(flops=0, bytes_accessed=8 * operands[0].size, transcendentals=0),
        name=name,
    )(*operands)


def add_kernel(*refs):
    total = refs[0][...].astype(F32)
    for ref in refs[1:-1]:
        total = total + ref[...].astype(F32)
    refs[-1][...] = total.astype(BF16)


def add(rows, *terms):
    width = terms[0][0].shape[1]

    def block(index):
        return pl.BlockSpec((rows, width), lambda i: (index, 0))

    return pl.pallas_call(
        add_kernel,
        grid=(1,),
        out_shape=jax.ShapeDtypeStruct((rows, width), BF16),
        in_specs=[block(index) for _, index in terms],
        out_specs=block(0),
        compiler_params=params(),
        cost_estimate=pl.CostEstimate(
            flops=rows * width * len(terms), bytes_accessed=2 * rows * width * (len(terms) + 1), transcendentals=0
        ),
        name="add",
    )(*[array for array, _ in terms])


def body(
    req_size,
    exp_size,
    attn_out,
    residual,
    out_weight,
    norm_gain,
    expert_ids,
    gate_weights,
    expert_gate,
    expert_up,
    expert_down,
    shared_gate,
    shared_up,
    shared_down,
):
    rows, width = attn_out.shape
    half = width // 2
    part = half // req_size
    topk = expert_ids.shape[1]
    wrows = out_weight.shape[0]
    capacity = min(rows, 3 * rows * topk // (2 * exp_size))
    slots = -(-2 * capacity // 16) * 16
    chips = exp_size // 2
    depth = chips // 2
    order = ring_order(chips)
    me = lax.axis_index("exp")
    request = lax.axis_index("req")
    here = jnp.stack([me, me % 2, lax.axis_index("req")]).astype(jnp.int32)
    ring = jnp.asarray([order.index(q) for q in range(chips)] + order, jnp.int32)

    steps = [(order[i], order[(i + 1) % chips]) for i in range(chips)]
    ahead = [(2 * a + c, 2 * b + c) for a, b in steps for c in range(2)]
    behind = [(b, a) for a, b in ahead]

    def to_ahead(x):
        return lax.ppermute(x, "exp", ahead)

    def to_behind(x):
        return lax.ppermute(x, "exp", behind)

    def to_core(x):
        return lax.ppermute(x, "exp", [(d, d ^ 1) for d in range(exp_size)])

    def to_request(x, shift, swap=0):
        pairs = [
            (i * exp_size + d, ((i + shift) % req_size) * exp_size + (d ^ swap))
            for i in range(req_size)
            for d in range(exp_size)
        ]
        return lax.ppermute(x, ("req", "exp"), pairs)

    weight_own, weight_sent = prepare(part, here, expert_ids.T, gate_weights.T, out_weight)
    weight = join(here, weight_own, to_core(weight_sent))
    low = high = weight
    pairs = []
    for _ in range(1, depth):
        low, high = to_ahead(low), to_behind(high)
        pairs.append((low, high))
    cut = wrows + TABLE_ROWS
    last = [to_ahead(low[:cut]), to_behind(high[cut:])]

    weight, attn_out, residual = lax.optimization_barrier((weight, attn_out, residual))
    packed = pack(req_size, part, here, attn_out, residual)
    visits = [packed[0]] + [to_request(packed[shift], shift) for shift in range(1, req_size)]
    passed = min(1, depth - 2)
    pairs[passed], visits[1:] = lax.optimization_barrier((pairs[passed], visits[1:]))
    visits += [to_core(v) for v in visits]

    early = [weight] + [w for pair in pairs[:-1] for w in pair]
    late = last + list(pairs[-1])
    tabs_early = tables(wrows, slots, topk, rows, here, [1] * (chips - 3), early)
    whole = early + list(pairs[-1])
    places = [(0, 1)] + [(side * k, 1) for k in range(1, depth) for side in (-1, 1)]
    (acc,) = proj(wrows, places, here, ring, visits, whole)
    acc, tabs_early = lax.optimization_barrier((acc, tabs_early))
    product = proj(wrows, [(depth, 2)], here, ring, visits, last, acc)
    tabs_late = tables(wrows, slots, topk, rows, here, [2, 1, 1], late)

    got = {}
    for shift in reversed(range(req_size)):
        for swap in range(2):
            piece = product[swap * req_size + shift]
            if shift == 0:
                got[shift, swap] = piece if swap == 0 else to_core(piece)
            else:
                got[shift, swap] = to_request(piece, req_size - shift, swap)
    near = beside(here, [got[0, 0], got[0, 1]])
    far, tabs_late = lax.optimization_barrier(
        ([got[place, swap] for place in range(1, req_size) for swap in range(2)], tabs_late)
    )
    far = beside(here, far)
    gain = norm_gain.reshape(1, width)
    weights = [expert_gate[0], expert_up[0], expert_down[0]]

    lows, highs = [to_ahead(near)], [to_behind(near)]
    lows, highs, far = lax.optimization_barrier((lows, highs, far))
    lows.append(to_ahead(far))
    highs.append(to_behind(far))
    own_rows = weave(req_size, here, [near, far])
    results = {0: expert(0, 1, tabs_early, gain, weights, [own_rows, to_core(own_rows)])}
    lows, highs, results[0] = lax.optimization_barrier((lows, highs, results[0]))
    low, high = weave(req_size, here, lows), weave(req_size, here, highs)
    shared_rows = [own_rows]
    for shift in range(1, req_size):
        shared_rows.append(to_request(own_rows, shift))
    for k in range(1, depth):
        if k > 1:
            low, high, results[k - 1] = lax.optimization_barrier((low, high, results[k - 1]))
        if k == depth - 1:
            low, high, shared_rows = lax.optimization_barrier((low, high, shared_rows))
        first, tabs = (2 * k - 1, tabs_early) if k < depth - 1 else (1, tabs_late)
        results[k] = expert(first, 2, tabs, gain, weights, [low, to_core(low), high, to_core(high)])
        if k < depth - 1:
            low, high = to_ahead(low), to_behind(high)
        else:
            low, high = to_ahead(low[: rows // 2]), to_behind(high[rows // 2 :])
    low, high, results[depth - 1] = lax.optimization_barrier((low, high, results[depth - 1]))
    results[depth] = expert(0, 1, tabs_late, gain, weights, [low, high, to_core(low), to_core(high)])

    shared_rows, results[depth] = lax.optimization_barrier((shared_rows, results[depth]))
    shared = shared_expert(gain, [shared_gate.T, shared_up.T, shared_down.T], shared_rows)

    cut = rows // 2
    low, high = [None, None], [None, None]
    for k in range(depth - 1, 0, -1):
        (low_mine, high_mine), theirs = results[k]
        came = to_core(theirs)

        def send_low(chunk):
            terms = [(low_mine, chunk), (came, chunk)] + [(low[chunk], 0)] * (low[chunk] is not None)
            low[chunk] = to_behind(add(cut, *terms))

        def send_high(chunk):
            terms = [(high_mine, chunk), (came, 2 + chunk)] + [(high[chunk], 0)] * (high[chunk] is not None)
            high[chunk] = to_ahead(add(cut, *terms))

        if k == depth - 1:
            send_low(0)
            send_high(1)
            results[depth], low[0], high[1] = lax.optimization_barrier((results[depth], low[0], high[1]))
            (mine,), theirs = results[depth]
            far = to_core(theirs)
            low[1] = to_behind(add(cut, (mine, 1), (far, 1)))
            high[0] = to_ahead(add(cut, (mine, 0), (far, 0)))
            send_low(1)
            send_high(0)
            continue
        if k == depth - 2:
            low[1], shared = lax.optimization_barrier((low[1], shared))
        for chunk in range(2):
            send_low(chunk)
            send_high(1 - chunk)
    (mine,), theirs = results[0]
    backs = [to_request(shared[shift], req_size - shift) for shift in range(1, req_size)]
    terms = [shared[0], own_rows, mine, to_core(theirs)] + backs
    base = plain_call(base_kernel, "base", jax.ShapeDtypeStruct((rows, width), F32), terms)
    return plain_call(
        functools.partial(final_kernel, 2), "final", jax.ShapeDtypeStruct((rows, width), BF16), [base] + low + high
    )


def solution(mesh):
    return jax.shard_map(
        functools.partial(body, mesh.shape["req"], mesh.shape["exp"]),
        mesh=mesh,
        in_specs=(
            P(("req", "exp"), None),
            P(("req", "exp"), None),
            P("exp", None),
            P(),
            P(("req", "exp"), None),
            P(("req", "exp"), None),
            P("exp", None, None),
            P("exp", None, None),
            P("exp", None, None),
            P(None, "req"),
            P(None, "req"),
            P(None, "req"),
        ),
        out_specs=P(("req", "exp"), None),
        check_vma=False,
    )
```

profile of v0, /device:TPU:0, one launch (start us, length us, event | category | flops | bytes accessed | tf_op | source)
XLA Modules:
  0.0 166.1 jit_solution(15124526604686130204)
XLA Ops:
  0.1 1.6 prepare.1
  2.2 1.0 collective-permute-done.other_ref
  3.8 2.2 %pack.1 = (bf16[128,3072]{1,0:T(8,128)(2,1)S(1)}, bf16[128,3072]{1,0:T(8,128)(2,1)S(1)}) custom-call(s32[3]{0:T(128)S(1)} %pad_add_fusion.where_ref, bf16[128,2048]{1,0:T(8,128)(2,1)} %attn_hbm, bf16[128,2048]{1,0:T(8,128)(2,1)} %residual_hbm), custom_call_target="tpu_custom_call" | custom-call | bytes 2097152 | tf_op jit(solution)/shard_map/pack/pallas_call | solution.py:144
  6.0 2.9 %collective-permute-start.5 = (bf16[128,3072]{1,0:T(8,128)(2,1)S(1)}, bf16[128,3072]{1,0:T(8,128)(2,1)S(1)}, u32[]{:S(2)}, u32[]{:S(2)}) collective-permute-start(bf16[128,3072]{1,0:T(8,128)(2,1)S(1)} %get-tuple-element.93), channel_id=1, source_target_pairs={{0,16},{1,17},{2,18},{3,19},{4,20},{5,21},{6,22},{7,23},{8,24},{9,... | collective-permute-start | bytes 2359304 | tf_op jit(solution)/shard_map/ppermute | solution.py:525
  8.9 1.5 collective-permute-start.3
  10.9 6.8 %collective-permute-done.3.refs_6_.refs_2_ = bf16[288,512]{1,0:T(8,128)(2,1)S(1)} collective-permute-done((bf16[288,512]{1,0:T(8,128)(2,1)S(1)}, bf16[288,512]{1,0:T(8,128)(2,1)S(1)}, u32[]{:S(2)}, u32[]{:S(2)}) %collective-permute-start.3) | collective-permute-done | bytes 294944 | tf_op jit(solution)/shard_map/ppermute | solution.py:514
  17.7 1.5 collective-permute-start.4
  19.7 5.9 %collective-permute-done.4.refs_8_.refs_4_ = bf16[288,512]{1,0:T(8,128)(2,1)S(1)} collective-permute-done((bf16[288,512]{1,0:T(8,128)(2,1)S(1)}, bf16[288,512]{1,0:T(8,128)(2,1)S(1)}, u32[]{:S(2)}, u32[]{:S(2)}) %collective-permute-start.4) | collective-permute-done | bytes 294944 | tf_op jit(solution)/shard_map/ppermute | solution.py:514
  25.6 1.2 collective-permute-done.2.refs_7_.refs_3_
  26.8 1.7 %collective-permute-start.10 = (bf16[288,512]{1,0:T(8,128)(2,1)S(1)}, bf16[288,512]{1,0:T(8,128)(2,1)S(1)}, u32[]{:S(2)}, u32[]{:S(2)}) collective-permute-start(bf16[288,512]{1,0:T(8,128)(2,1)S(1)} %collective-permute-done.4.refs_8_.refs_4_), channel_id=1, source_target_pairs={{4,0},{5,1},{8,4},{9,5},{12,8},{13,9},{14,12},{15,13},{10,14},{11,... | collective-permute-start | bytes 884744 | tf_op jit(solution)/shard_map/ppermute | solution.py:514
  28.9 1.5 tables.2
  30.3 5.9 %collective-permute-done.10.refs_10_.refs_3_ = bf16[288,512]{1,0:T(8,128)(2,1)S(1)} collective-permute-done((bf16[288,512]{1,0:T(8,128)(2,1)S(1)}, bf16[288,512]{1,0:T(8,128)(2,1)S(1)}, u32[]{:S(2)}, u32[]{:S(2)}) %collective-permute-start.10) | collective-permute-done | bytes 294944 | tf_op jit(solution)/shard_map/ppermute | solution.py:514
  36.3 1.7 %collective-permute-start.11 = (bf16[144,512]{1,0:T(8,128)(2,1)S(1)}, bf16[144,512]{1,0:T(8,128)(2,1)S(1)}, u32[]{:S(2)}, u32[]{:S(2)}) collective-permute-start(bf16[144,512]{1,0:T(8,128)(2,1)S(1)} %slice.17), channel_id=1, source_target_pairs={{4,0},{5,1},{8,4},{9,5},{12,8},{13,9},{14,12},{15,13},{10,14},{11,... | collective-permute-start | bytes 442376 | tf_op jit(solution)/shard_map/ppermute | solution.py:514
  38.5 0.8 copy-done.2
  39.3 1.6 proj_part.1.refs_6_
  41.0 0.8 collective-permute-done.11.refs_5_.refs_1_
  41.8 1.5 collective-permute-done.9.refs_4_.refs_0_
  43.3 0.8 proj_final.1
  44.2 1.3 collective-permute-done.12.refs_1_
  46.1 1.6 collective-permute-start.14
  48.2 1.5 collective-permute-start.15
  49.7 1.1 tables.3
  50.8 2.9 %collective-permute-done.15.refs_0_ = bf16[128,512]{1,0:T(8,128)(2,1)S(1)} collective-permute-done((bf16[128,512]{1,0:T(8,128)(2,1)S(1)}, bf16[128,512]{1,0:T(8,128)(2,1)S(1)}, u32[]{:S(2)}, u32[]{:S(2)}) %collective-permute-start.15) | collective-permute-done | bytes 131104 | tf_op jit(solution)/shard_map/ppermute | solution.py:525
  53.7 1.7 %collective-permute-done.16.refs_1_ = bf16[128,512]{1,0:T(8,128)(2,1)S(1)} collective-permute-done((bf16[128,512]{1,0:T(8,128)(2,1)S(1)}, bf16[128,512]{1,0:T(8,128)(2,1)S(1)}, u32[]{:S(2)}, u32[]{:S(2)}) %collective-permute-start.16) | collective-permute-done | bytes 131104 | tf_op jit(solution)/shard_map/ppermute | solution.py:525
  57.2 1.6 collective-permute-start.18
  59.3 4.2 %expert.5 = (bf16[128,2048]{1,0:T(8,128)(2,1)S(1)}, bf16[128,2048]{1,0:T(8,128)(2,1)S(1)}) custom-call(f32[1,2048]{1,0:T(1,128)S(1)} %bitcast.31, bf16[5,144,256]{2,1,0:T(8,128)(2,1)S(1)} %get-tuple-element.114.pick_ref, bf16[5,256,144]{2,1,0:T(8,128)(2,1)S(1)} %get-tuple-element.115.put_ref, f32[5,144,1]{2,1,0:T(8,128)S(1)} %get-tuple-element.116.factor_ref, ...), custom_call_target="tpu_custom_call" | custom-call | flops 4982833152 | bytes 4194304 | tf_op jit(solution)/shard_map/expert/pallas_call | solution.py:338
  63.5 2.0 %collective-permute-done.18.refs_1_ = bf16[128,1024]{1,0:T(8,128)(2,1)S(1)} collective-permute-done((bf16[128,1024]{1,0:T(8,128)(2,1)S(1)}, bf16[128,1024]{1,0:T(8,128)(2,1)S(1)}, u32[]{:S(2)}, u32[]{:S(2)}) %collective-permute-start.18) | collective-permute-done | bytes 262176 | tf_op jit(solution)/shard_map/ppermute | solution.py:514
  65.5 1.3 collective-permute-done.17.refs_1_
  68.6 1.6 collective-permute-start.21
  70.6 7.2 %expert.6 = (bf16[128,2048]{1,0:T(8,128)(2,1)S(1)}, bf16[128,2048]{1,0:T(8,128)(2,1)S(1)}, bf16[256,2048]{1,0:T(8,128)(2,1)S(1)}) custom-call(f32[1,2048]{1,0:T(1,128)S(1)} %bitcast.32, bf16[5,144,256]{2,1,0:T(8,128)(2,1)S(1)} %get-tuple-element.114.pick_ref, bf16[5,256,144]{2,1,0:T(8,128)(2,1)S(1)} %get-tuple-element.115.put_ref, ...), custom_call_target="tpu_custom_call" | custom-call | flops 9965666304 | bytes 8388608 | tf_op jit(solution)/shard_map/expert/pallas_call | solution.py:338
  77.9 4.6 %collective-permute-done.21.refs_2_ = bf16[128,2048]{1,0:T(8,128)(2,1)S(1)} collective-permute-done((bf16[128,2048]{1,0:T(8,128)(2,1)S(1)}, bf16[128,2048]{1,0:T(8,128)(2,1)S(1)}, u32[]{:S(2)}, u32[]{:S(2)}) %collective-permute-start.21) | collective-permute-done | bytes 524320 | tf_op jit(solution)/shard_map/ppermute | solution.py:514
  82.5 1.3 collective-permute-done.20.refs_0_
  84.3 1.5 collective-permute-start.28
  86.2 1.6 collective-permute-start.25
  87.8 7.2 %expert.7 = (bf16[128,2048]{1,0:T(8,128)(2,1)S(1)}, bf16[128,2048]{1,0:T(8,128)(2,1)S(1)}, bf16[256,2048]{1,0:T(8,128)(2,1)S(1)}) custom-call(f32[1,2048]{1,0:T(1,128)S(1)} %bitcast.33, bf16[5,144,256]{2,1,0:T(8,128)(2,1)S(1)} %get-tuple-element.114.pick_ref, bf16[5,256,144]{2,1,0:T(8,128)(2,1)S(1)} %get-tuple-element.115.put_ref, ...), custom_call_target="tpu_custom_call" | custom-call | flops 9965666304 | bytes 8388608 | tf_op jit(solution)/shard_map/expert/pallas_call | solution.py:338
  95.0 4.3 %collective-permute-done.24.refs_0_ = bf16[128,2048]{1,0:T(8,128)(2,1)S(1)} collective-permute-done((bf16[128,2048]{1,0:T(8,128)(2,1)S(1)}, bf16[128,2048]{1,0:T(8,128)(2,1)S(1)}, u32[]{:S(2)}, u32[]{:S(2)}) %collective-permute-start.24) | collective-permute-done | bytes 524320 | tf_op jit(solution)/shard_map/ppermute | solution.py:511
  100.1 1.6 collective-permute-start.30
  102.2 7.2 %expert.8 = (bf16[128,2048]{1,0:T(8,128)(2,1)S(1)}, bf16[128,2048]{1,0:T(8,128)(2,1)S(1)}, bf16[256,2048]{1,0:T(8,128)(2,1)S(1)}) custom-call(f32[1,2048]{1,0:T(1,128)S(1)} %bitcast.34, bf16[3,144,256]{2,1,0:T(8,128)(2,1)S(1)} %get-tuple-element.135.pick_ref, bf16[3,256,144]{2,1,0:T(8,128)(2,1)S(1)} %get-tuple-element.136.put_ref, ...), custom_call_target="tpu_custom_call" | custom-call | flops 9965666304 | bytes 8388608 | tf_op jit(solution)/shard_map/expert/pallas_call | solution.py:338
  110.7 1.6 collective-permute-done.33.refs_1_
  112.4 1.5 collective-permute-start.36
  113.9 0.6 collective-permute-start.37
  114.6 4.2 %expert.9 = (bf16[128,2048]{1,0:T(8,128)(2,1)S(1)}, bf16[128,2048]{1,0:T(8,128)(2,1)S(1)}) custom-call(f32[1,2048]{1,0:T(1,128)S(1)} %bitcast.35, bf16[3,144,256]{2,1,0:T(8,128)(2,1)S(1)} %get-tuple-element.135.pick_ref, bf16[3,256,144]{2,1,0:T(8,128)(2,1)S(1)} %get-tuple-element.136.put_ref, f32[3,144,1]{2,1,0:T(8,128)S(1)} %get-tuple-element.137.factor_ref, ...), custom_call_target="tpu_custom_call" | custom-call | flops 4982833152 | bytes 4194304 | tf_op jit(solution)/shard_map/expert/pallas_call | solution.py:338
  118.8 2.0 %collective-permute-done.36.refs_2_ = bf16[64,2048]{1,0:T(8,128)(2,1)S(1)} collective-permute-done((bf16[64,2048]{1,0:T(8,128)(2,1)S(1)}, bf16[64,2048]{1,0:T(8,128)(2,1)S(1)}, u32[]{:S(2)}, u32[]{:S(2)}) %collective-permute-start.36) | collective-permute-done | bytes 262176 | tf_op jit(solution)/shard_map/ppermute | solution.py:514
  120.8 1.3 collective-permute-done.37.refs_2_
  122.6 1.4 collective-permute-done.38.refs_1_
  124.0 1.5 collective-permute-start.39
  125.6 0.7 collective-permute-start.49
  126.3 1.5 collective-permute-start.45
  127.8 5.4 %collective-permute-done.39.refs_2_ = bf16[64,2048]{1,0:T(8,128)(2,1)S(1)} collective-permute-done((bf16[64,2048]{1,0:T(8,128)(2,1)S(1)}, bf16[64,2048]{1,0:T(8,128)(2,1)S(1)}, u32[]{:S(2)}, u32[]{:S(2)}) %collective-permute-start.39) | collective-permute-done | bytes 262176 | tf_op jit(solution)/shard_map/ppermute | solution.py:514
  133.3 1.5 collective-permute-start.40
  134.9 0.9 collective-permute-start.50
  135.8 4.8 %shared.1 = (f32[128,2048]{1,0:T(8,128)S(1)}, bf16[128,2048]{1,0:T(8,128)(2,1)S(1)}) custom-call(f32[1,2048]{1,0:T(1,128)S(1)} %bitcast.36, bf16[704,2048]{1,0:T(8,128)(2,1)} %bitcast.39, bf16[704,2048]{1,0:T(8,128)(2,1)} %bitcast.40, bf16[704,2048]{1,0:T(8,128)(2,1)} %bitcast.41, bf16[128,2048]{1,0:T(8,128)(2,1)S(1)} %weave.3.refs_0_.refs_1_, ...), custom_call_target="tpu_custom_call" | custom-call | flops 4429185024 | bytes 10747904 | tf_op jit(solution)/shard_map/shared/pallas_call | solution.py:399
  140.8 0.9 collective-permute-done.50.refs_2_
  141.7 0.6 collective-permute-start.53
  142.4 1.3 collective-permute-done.40.refs_2_
  144.9 1.6 collective-permute-start.47
  146.6 4.0 %collective-permute-done.53.refs_2_ = bf16[64,2048]{1,0:T(8,128)(2,1)S(1)} collective-permute-done((bf16[64,2048]{1,0:T(8,128)(2,1)S(1)}, bf16[64,2048]{1,0:T(8,128)(2,1)S(1)}, u32[]{:S(2)}, u32[]{:S(2)}) %collective-permute-start.53) | collective-permute-done | bytes 262176 | tf_op jit(solution)/shard_map/ppermute | solution.py:511
  150.7 3.0 %collective-permute-done.51.refs_2_ = bf16[64,2048]{1,0:T(8,128)(2,1)S(1)} collective-permute-done((bf16[64,2048]{1,0:T(8,128)(2,1)S(1)}, bf16[64,2048]{1,0:T(8,128)(2,1)S(1)}, u32[]{:S(2)}, u32[]{:S(2)}) %collective-permute-start.51) | collective-permute-done | bytes 262176 | tf_op jit(solution)/shard_map/ppermute | solution.py:511
  154.4 0.6 collective-permute-start.52
  155.1 1.5 collective-permute-start.48
  157.4 2.4 %collective-permute-done.46.refs_0_ = bf16[64,2048]{1,0:T(8,128)(2,1)S(1)} collective-permute-done((bf16[64,2048]{1,0:T(8,128)(2,1)S(1)}, bf16[64,2048]{1,0:T(8,128)(2,1)S(1)}, u32[]{:S(2)}, u32[]{:S(2)}) %collective-permute-start.46) | collective-permute-done | bytes 262176 | tf_op jit(solution)/shard_map/ppermute | solution.py:514
  159.8 2.5 %collective-permute-done.54.refs_3_ = bf16[64,2048]{1,0:T(8,128)(2,1)S(1)} collective-permute-done((bf16[64,2048]{1,0:T(8,128)(2,1)S(1)}, bf16[64,2048]{1,0:T(8,128)(2,1)S(1)}, u32[]{:S(2)}, u32[]{:S(2)}) %collective-permute-start.54) | collective-permute-done | bytes 262176 | tf_op jit(solution)/shard_map/ppermute | solution.py:511
  162.3 2.8 %collective-permute-done.52.refs_2_ = bf16[64,2048]{1,0:T(8,128)(2,1)S(1)} collective-permute-done((bf16[64,2048]{1,0:T(8,128)(2,1)S(1)}, bf16[64,2048]{1,0:T(8,128)(2,1)S(1)}, u32[]{:S(2)}, u32[]{:S(2)}) %collective-permute-start.52) | collective-permute-done | bytes 262176 | tf_op jit(solution)/shard_map/ppermute | solution.py:511
  165.1 1.0 final.1
  (101 shorter events, 16.1 us)
Async XLA Ops:
  1.7 1.5 collective-permute-start
  3.8 55.5 %copy-start = (bf16[1,1408,2048]{2,1,0:T(8,128)(2,1)S(1)}, bf16[1,1408,2048]{2,1,0:T(8,128)(2,1)}, u32[]{:S(2)}) copy-start(bf16[1,1408,2048]{2,1,0:T(8,128)(2,1)} %param.21) | copy-start | bytes 17301508
  6.0 20.9 %collective-permute-start.5 = (bf16[128,3072]{1,0:T(8,128)(2,1)S(1)}, bf16[128,3072]{1,0:T(8,128)(2,1)S(1)}, u32[]{:S(2)}, u32[]{:S(2)}) collective-permute-start(bf16[128,3072]{1,0:T(8,128)(2,1)S(1)} %get-tuple-element.93), channel_id=1, source_target_pairs={{0,16},{1,17},{2,18},{3,19},{4,20},{5,21},{6,22},{7,23},{8,24},{9,... | collective-permute-start | bytes 2359304 | tf_op jit(solution)/shard_map/ppermute | solution.py:525
  8.9 8.8 %collective-permute-start.3 = (bf16[288,512]{1,0:T(8,128)(2,1)S(1)}, bf16[288,512]{1,0:T(8,128)(2,1)S(1)}, u32[]{:S(2)}, u32[]{:S(2)}) collective-permute-start(bf16[288,512]{1,0:T(8,128)(2,1)S(1)} %join.1.refs_4_.refs_0_), channel_id=1, source_target_pairs={{4,0},{5,1},{8,4},{9,5},{12,8},{13,9},{14,12},{15,13},{10,14},{11,... | collective-permute-start | bytes 884744 | tf_op jit(solution)/shard_map/ppermute | solution.py:514
  10.4 8.8 %collective-permute-start.1 = (bf16[288,512]{1,0:T(8,128)(2,1)S(1)}, bf16[288,512]{1,0:T(8,128)(2,1)S(1)}, u32[]{:S(2)}, u32[]{:S(2)}) collective-permute-start(bf16[288,512]{1,0:T(8,128)(2,1)S(1)} %join.1.refs_4_.refs_0_), channel_id=1, source_target_pairs={{0,4},{1,5},{4,8},{5,9},{8,12},{9,13},{12,14},{13,15},{14,10},{15,... | collective-permute-start | bytes 884744 | tf_op jit(solution)/shard_map/ppermute | solution.py:511
  17.7 7.9 %collective-permute-start.4 = (bf16[288,512]{1,0:T(8,128)(2,1)S(1)}, bf16[288,512]{1,0:T(8,128)(2,1)S(1)}, u32[]{:S(2)}, u32[]{:S(2)}) collective-permute-start(bf16[288,512]{1,0:T(8,128)(2,1)S(1)} %collective-permute-done.3.refs_6_.refs_2_), channel_id=1, source_target_pairs={{4,0},{5,1},{8,4},{9,5},{12,8},{13,9},{14,12},{15,13},{10,14},{11,... | collective-permute-start | bytes 884744 | tf_op jit(solution)/shard_map/ppermute | solution.py:514
  19.2 7.6 %collective-permute-start.2 = (bf16[288,512]{1,0:T(8,128)(2,1)S(1)}, bf16[288,512]{1,0:T(8,128)(2,1)S(1)}, u32[]{:S(2)}, u32[]{:S(2)}) collective-permute-start(bf16[288,512]{1,0:T(8,128)(2,1)S(1)} %collective-permute-done.1.refs_5_.refs_1_), channel_id=1, source_target_pairs={{0,4},{1,5},{4,8},{5,9},{8,12},{9,13},{12,14},{13,15},{14,10},{15,... | collective-permute-start | bytes 884744 | tf_op jit(solution)/shard_map/ppermute | solution.py:511
  19.7 18.8 %collective-permute-start.6 = (bf16[128,3072]{1,0:T(8,128)(2,1)S(1)}, bf16[128,3072]{1,0:T(8,128)(2,1)S(1)}, u32[]{:S(2)}, u32[]{:S(2)}) collective-permute-start(bf16[128,3072]{1,0:T(8,128)(2,1)S(1)} %get-tuple-element.92.refs_0_), channel_id=1, source_target_pairs={{0,1},{1,0},{2,3},{3,2},{4,5},{5,4},{6,7},{7,6},{8,9},{9,8},{10,11... | collective-permute-start | bytes 2359304 | tf_op jit(solution)/shard_map/ppermute | solution.py:517
  26.8 11.6 %collective-permute-start.7 = (bf16[128,3072]{1,0:T(8,128)(2,1)S(1)}, bf16[128,3072]{1,0:T(8,128)(2,1)S(1)}, u32[]{:S(2)}, u32[]{:S(2)}) collective-permute-start(bf16[128,3072]{1,0:T(8,128)(2,1)S(1)} %collective-permute-done.5.refs_1_), channel_id=1, source_target_pairs={{0,1},{1,0},{2,3},{3,2},{4,5},{5,4},{6,7},{7,6},{8,9},{9,8},{10,11... | collective-permute-start | bytes 2359304 | tf_op jit(solution)/shard_map/ppermute | solution.py:517
  26.8 9.4 %collective-permute-start.10 = (bf16[288,512]{1,0:T(8,128)(2,1)S(1)}, bf16[288,512]{1,0:T(8,128)(2,1)S(1)}, u32[]{:S(2)}, u32[]{:S(2)}) collective-permute-start(bf16[288,512]{1,0:T(8,128)(2,1)S(1)} %collective-permute-done.4.refs_8_.refs_4_), channel_id=1, source_target_pairs={{4,0},{5,1},{8,4},{9,5},{12,8},{13,9},{14,12},{15,13},{10,14},{11,... | collective-permute-start | bytes 884744 | tf_op jit(solution)/shard_map/ppermute | solution.py:514
  28.5 9.5 %collective-permute-start.8 = (bf16[288,512]{1,0:T(8,128)(2,1)S(1)}, bf16[288,512]{1,0:T(8,128)(2,1)S(1)}, u32[]{:S(2)}, u32[]{:S(2)}) collective-permute-start(bf16[288,512]{1,0:T(8,128)(2,1)S(1)} %collective-permute-done.2.refs_7_.refs_3_), channel_id=1, source_target_pairs={{0,4},{1,5},{4,8},{5,9},{8,12},{9,13},{12,14},{13,15},{14,10},{15,... | collective-permute-start | bytes 884744 | tf_op jit(solution)/shard_map/ppermute | solution.py:511
  28.9 30.4 %slice-start.2 = ((s8[5767168]{0:T(1024)(128)(4,1)}), s8[4194304]{0:T(1024)(128)(4,1)S(1)}, s32[]{:S(2)}) async-start(s8[5767168]{0:T(1024)(128)(4,1)} %bitcast.19), calls=%async_computation.2 | async-start | bytes 8388608
  36.2 23.0 %slice-start = ((s8[5767168]{0:T(1024)(128)(4,1)}), s8[4194304]{0:T(1024)(128)(4,1)S(1)}, s32[]{:S(2)}) async-start(s8[5767168]{0:T(1024)(128)(4,1)} %bitcast.12), calls=%async_computation | async-start | bytes 8388608
  36.3 5.5 %collective-permute-start.11 = (bf16[144,512]{1,0:T(8,128)(2,1)S(1)}, bf16[144,512]{1,0:T(8,128)(2,1)S(1)}, u32[]{:S(2)}, u32[]{:S(2)}) collective-permute-start(bf16[144,512]{1,0:T(8,128)(2,1)S(1)} %slice.17), channel_id=1, source_target_pairs={{4,0},{5,1},{8,4},{9,5},{12,8},{13,9},{14,12},{15,13},{10,14},{11,... | collective-permute-start | bytes 442376 | tf_op jit(solution)/shard_map/ppermute | solution.py:514
  38.0 21.2 %slice-start.1 = ((s8[5767168]{0:T(1024)(128)(4,1)}), s8[1572864]{0:T(1024)(128)(4,1)S(1)}, s32[]{:S(2)}) async-start(s8[5767168]{0:T(1024)(128)(4,1)} %bitcast.12), calls=%async_computation.1 | async-start | bytes 3145728
  38.0 21.2 %slice-start.3 = ((s8[5767168]{0:T(1024)(128)(4,1)}), s8[1572864]{0:T(1024)(128)(4,1)S(1)}, s32[]{:S(2)}) async-start(s8[5767168]{0:T(1024)(128)(4,1)} %bitcast.19), calls=%async_computation.3 | async-start | bytes 3145728
  38.0 21.2 %copy-start.1 = (f32[2048]{0:T(1024)S(1)}, f32[2048]{0:T(1024)}, u32[]{:S(2)}) copy-start(f32[2048]{0:T(1024)} %param.16) | copy-start | bytes 24580
  38.1 5.3 %collective-permute-start.9 = (bf16[144,512]{1,0:T(8,128)(2,1)S(1)}, bf16[144,512]{1,0:T(8,128)(2,1)S(1)}, u32[]{:S(2)}, u32[]{:S(2)}) collective-permute-start(bf16[144,512]{1,0:T(8,128)(2,1)S(1)} %slice.16), channel_id=1, source_target_pairs={{0,4},{1,5},{4,8},{5,9},{8,12},{9,13},{12,14},{13,15},{14,10},{15,... | collective-permute-start | bytes 442376 | tf_op jit(solution)/shard_map/ppermute | solution.py:511
  38.5 0.8 copy-start.2
  44.2 1.4 collective-permute-start.12
  46.1 9.9 %collective-permute-start.14 = (bf16[128,1024]{1,0:T(8,128)(2,1)S(1)}, bf16[128,1024]{1,0:T(8,128)(2,1)S(1)}, u32[]{:S(2)}, u32[]{:S(2)}) collective-permute-start(bf16[128,1024]{1,0:T(8,128)(2,1)S(1)} %beside.2.refs_0_), channel_id=1, source_target_pairs={{4,0},{5,1},{8,4},{9,5},{12,8},{13,9},{14,12},{15,13},{10,14},{11,... | collective-permute-start | bytes 786440 | tf_op jit(solution)/shard_map/ppermute | solution.py:514
  47.8 8.3 %collective-permute-start.13 = (bf16[128,1024]{1,0:T(8,128)(2,1)S(1)}, bf16[128,1024]{1,0:T(8,128)(2,1)S(1)}, u32[]{:S(2)}, u32[]{:S(2)}) collective-permute-start(bf16[128,1024]{1,0:T(8,128)(2,1)S(1)} %beside.2.refs_0_), channel_id=1, source_target_pairs={{0,4},{1,5},{4,8},{5,9},{8,12},{9,13},{12,14},{13,15},{14,10},{15,... | collective-permute-start | bytes 786440 | tf_op jit(solution)/shard_map/ppermute | solution.py:511
  48.2 5.5 %collective-permute-start.15 = (bf16[128,512]{1,0:T(8,128)(2,1)S(1)}, bf16[128,512]{1,0:T(8,128)(2,1)S(1)}, u32[]{:S(2)}, u32[]{:S(2)}) collective-permute-start(bf16[128,512]{1,0:T(8,128)(2,1)S(1)} %get-tuple-element.104), channel_id=1, source_target_pairs={{0,16},{1,17},{2,18},{3,19},{4,20},{5,21},{6,22},{7,23},{8,24},{9,... | collective-permute-start | bytes 393224 | tf_op jit(solution)/shard_map/ppermute | solution.py:525
  49.7 5.8 %collective-permute-start.16 = (bf16[128,512]{1,0:T(8,128)(2,1)S(1)}, bf16[128,512]{1,0:T(8,128)(2,1)S(1)}, u32[]{:S(2)}, u32[]{:S(2)}) collective-permute-start(bf16[128,512]{1,0:T(8,128)(2,1)S(1)} %get-tuple-element.105), channel_id=1, source_target_pairs={{0,17},{1,16},{2,19},{3,18},{4,21},{5,20},{6,23},{7,22},{8,25},{9,... | collective-permute-start | bytes 393224 | tf_op jit(solution)/shard_map/ppermute | solution.py:525
  56.7 2.6 %collective-permute-start.19 = (bf16[128,2048]{1,0:T(8,128)(2,1)S(1)}, bf16[128,2048]{1,0:T(8,128)(2,1)S(1)}, u32[]{:S(2)}, u32[]{:S(2)}) collective-permute-start(bf16[128,2048]{1,0:T(8,128)(2,1)S(1)} %weave.3.refs_0_.refs_1_), channel_id=1, source_target_pairs={{0,1},{1,0},{2,3},{3,2},{4,5},{5,4},{6,7},{7,6},{8,9},{9,8},{10,11... | collective-permute-start | bytes 1572872 | tf_op jit(solution)/shard_map/ppermute | solution.py:517
  57.2 8.3 %collective-permute-start.18 = (bf16[128,1024]{1,0:T(8,128)(2,1)S(1)}, bf16[128,1024]{1,0:T(8,128)(2,1)S(1)}, u32[]{:S(2)}, u32[]{:S(2)}) collective-permute-start(bf16[128,1024]{1,0:T(8,128)(2,1)S(1)} %beside.3.refs_1_), channel_id=1, source_target_pairs={{4,0},{5,1},{8,4},{9,5},{12,8},{13,9},{14,12},{15,13},{10,14},{11,... | collective-permute-start | bytes 786440 | tf_op jit(solution)/shard_map/ppermute | solution.py:514
  58.8 8.0 %collective-permute-start.17 = (bf16[128,1024]{1,0:T(8,128)(2,1)S(1)}, bf16[128,1024]{1,0:T(8,128)(2,1)S(1)}, u32[]{:S(2)}, u32[]{:S(2)}) collective-permute-start(bf16[128,1024]{1,0:T(8,128)(2,1)S(1)} %beside.3.refs_1_), channel_id=1, source_target_pairs={{0,4},{1,5},{4,8},{5,9},{8,12},{9,13},{12,14},{13,15},{14,10},{15,... | collective-permute-start | bytes 786440 | tf_op jit(solution)/shard_map/ppermute | solution.py:511
  67.4 3.3 %collective-permute-start.23 = (bf16[128,2048]{1,0:T(8,128)(2,1)S(1)}, bf16[128,2048]{1,0:T(8,128)(2,1)S(1)}, u32[]{:S(2)}, u32[]{:S(2)}) collective-permute-start(bf16[128,2048]{1,0:T(8,128)(2,1)S(1)} %weave.5.refs_2_), channel_id=1, source_target_pairs={{0,1},{1,0},{2,3},{3,2},{4,5},{5,4},{6,7},{7,6},{8,9},{9,8},{10,11... | collective-permute-start | bytes 1572872 | tf_op jit(solution)/shard_map/ppermute | solution.py:517
  68.0 2.6 %collective-permute-start.22 = (bf16[128,2048]{1,0:T(8,128)(2,1)S(1)}, bf16[128,2048]{1,0:T(8,128)(2,1)S(1)}, u32[]{:S(2)}, u32[]{:S(2)}) collective-permute-start(bf16[128,2048]{1,0:T(8,128)(2,1)S(1)} %weave.4.refs_0_), channel_id=1, source_target_pairs={{0,1},{1,0},{2,3},{3,2},{4,5},{5,4},{6,7},{7,6},{8,9},{9,8},{10,11... | collective-permute-start | bytes 1572872 | tf_op jit(solution)/shard_map/ppermute | solution.py:517
  68.6 13.9 %collective-permute-start.21 = (bf16[128,2048]{1,0:T(8,128)(2,1)S(1)}, bf16[128,2048]{1,0:T(8,128)(2,1)S(1)}, u32[]{:S(2)}, u32[]{:S(2)}) collective-permute-start(bf16[128,2048]{1,0:T(8,128)(2,1)S(1)} %weave.5.refs_2_), channel_id=1, source_target_pairs={{4,0},{5,1},{8,4},{9,5},{12,8},{13,9},{14,12},{15,13},{10,14},{11,... | collective-permute-start | bytes 1572872 | tf_op jit(solution)/shard_map/ppermute | solution.py:514
  70.2 13.6 %collective-permute-start.20 = (bf16[128,2048]{1,0:T(8,128)(2,1)S(1)}, bf16[128,2048]{1,0:T(8,128)(2,1)S(1)}, u32[]{:S(2)}, u32[]{:S(2)}) collective-permute-start(bf16[128,2048]{1,0:T(8,128)(2,1)S(1)} %weave.4.refs_0_), channel_id=1, source_target_pairs={{0,4},{1,5},{4,8},{5,9},{8,12},{9,13},{12,14},{13,15},{14,10},{15,... | collective-permute-start | bytes 1572872 | tf_op jit(solution)/shard_map/ppermute | solution.py:511
  83.8 4.0 %collective-permute-start.26 = (bf16[128,2048]{1,0:T(8,128)(2,1)S(1)}, bf16[128,2048]{1,0:T(8,128)(2,1)S(1)}, u32[]{:S(2)}, u32[]{:S(2)}) collective-permute-start(bf16[128,2048]{1,0:T(8,128)(2,1)S(1)} %collective-permute-done.20.refs_0_), channel_id=1, source_target_pairs={{0,1},{1,0},{2,3},{3,2},{4,5},{5,4},{6,7},{7,6},{8,9},{9,8},{10,11... | collective-permute-start | bytes 1572872 | tf_op jit(solution)/shard_map/ppermute | solution.py:517
  83.8 4.0 %collective-permute-start.27 = (bf16[128,2048]{1,0:T(8,128)(2,1)S(1)}, bf16[128,2048]{1,0:T(8,128)(2,1)S(1)}, u32[]{:S(2)}, u32[]{:S(2)}) collective-permute-start(bf16[128,2048]{1,0:T(8,128)(2,1)S(1)} %collective-permute-done.21.refs_2_), channel_id=1, source_target_pairs={{0,1},{1,0},{2,3},{3,2},{4,5},{5,4},{6,7},{7,6},{8,9},{9,8},{10,11... | collective-permute-start | bytes 1572872 | tf_op jit(solution)/shard_map/ppermute | solution.py:517
  84.3 15.2 %collective-permute-start.28 = (bf16[128,2048]{1,0:T(8,128)(2,1)S(1)}, bf16[128,2048]{1,0:T(8,128)(2,1)S(1)}, u32[]{:S(2)}, u32[]{:S(2)}) collective-permute-start(bf16[128,2048]{1,0:T(8,128)(2,1)S(1)} %weave.3.refs_0_.refs_1_), channel_id=1, source_target_pairs={{0,16},{1,17},{2,18},{3,19},{4,20},{5,21},{6,22},{7,23},{8,24},{9,... | collective-permute-start | bytes 1572872 | tf_op jit(solution)/shard_map/ppermute | solution.py:525
  85.8 13.6 %collective-permute-start.24 = (bf16[128,2048]{1,0:T(8,128)(2,1)S(1)}, bf16[128,2048]{1,0:T(8,128)(2,1)S(1)}, u32[]{:S(2)}, u32[]{:S(2)}) collective-permute-start(bf16[128,2048]{1,0:T(8,128)(2,1)S(1)} %collective-permute-done.20.refs_0_), channel_id=1, source_target_pairs={{0,4},{1,5},{4,8},{5,9},{8,12},{9,13},{12,14},{13,15},{14,10},{15,... | collective-permute-start | bytes 1572872 | tf_op jit(solution)/shard_map/ppermute | solution.py:511
  86.2 13.3 %collective-permute-start.25 = (bf16[128,2048]{1,0:T(8,128)(2,1)S(1)}, bf16[128,2048]{1,0:T(8,128)(2,1)S(1)}, u32[]{:S(2)}, u32[]{:S(2)}) collective-permute-start(bf16[128,2048]{1,0:T(8,128)(2,1)S(1)} %collective-permute-done.21.refs_2_), channel_id=1, source_target_pairs={{4,0},{5,1},{8,4},{9,5},{12,8},{13,9},{14,12},{15,13},{10,14},{11,... | collective-permute-start | bytes 1572872 | tf_op jit(solution)/shard_map/ppermute | solution.py:514
  99.5 2.6 %collective-permute-start.31 = (bf16[128,2048]{1,0:T(8,128)(2,1)S(1)}, bf16[128,2048]{1,0:T(8,128)(2,1)S(1)}, u32[]{:S(2)}, u32[]{:S(2)}) collective-permute-start(bf16[128,2048]{1,0:T(8,128)(2,1)S(1)} %collective-permute-done.24.refs_0_), channel_id=1, source_target_pairs={{0,1},{1,0},{2,3},{3,2},{4,5},{5,4},{6,7},{7,6},{8,9},{9,8},{10,11... | collective-permute-start | bytes 1572872 | tf_op jit(solution)/shard_map/ppermute | solution.py:517
  99.5 2.7 %collective-permute-start.32 = (bf16[128,2048]{1,0:T(8,128)(2,1)S(1)}, bf16[128,2048]{1,0:T(8,128)(2,1)S(1)}, u32[]{:S(2)}, u32[]{:S(2)}) collective-permute-start(bf16[128,2048]{1,0:T(8,128)(2,1)S(1)} %collective-permute-done.25.refs_2_), channel_id=1, source_target_pairs={{0,1},{1,0},{2,3},{3,2},{4,5},{5,4},{6,7},{7,6},{8,9},{9,8},{10,11... | collective-permute-start | bytes 1572872 | tf_op jit(solution)/shard_map/ppermute | solution.py:517
  100.1 9.3 %collective-permute-start.30 = (bf16[64,2048]{1,0:T(8,128)(2,1)S(1)}, bf16[64,2048]{1,0:T(8,128)(2,1)S(1)}, u32[]{:S(2)}, u32[]{:S(2)}) collective-permute-start(bf16[64,2048]{1,0:T(8,128)(2,1)S(1)} %slice.15), channel_id=1, source_target_pairs={{4,0},{5,1},{8,4},{9,5},{12,8},{13,9},{14,12},{15,13},{10,14},{11,... | collective-permute-start | bytes 786440 | tf_op jit(solution)/shard_map/ppermute | solution.py:514
  101.7 7.9 %collective-permute-start.29 = (bf16[64,2048]{1,0:T(8,128)(2,1)S(1)}, bf16[64,2048]{1,0:T(8,128)(2,1)S(1)}, u32[]{:S(2)}, u32[]{:S(2)}) collective-permute-start(bf16[64,2048]{1,0:T(8,128)(2,1)S(1)} %slice.14), channel_id=1, source_target_pairs={{0,4},{1,5},{4,8},{5,9},{8,12},{9,13},{12,14},{13,15},{14,10},{15,... | collective-permute-start | bytes 786440 | tf_op jit(solution)/shard_map/ppermute | solution.py:511
  109.6 2.7 %collective-permute-start.33 = (bf16[256,2048]{1,0:T(8,128)(2,1)S(1)}, bf16[256,2048]{1,0:T(8,128)(2,1)S(1)}, u32[]{:S(2)}, u32[]{:S(2)}) collective-permute-start(bf16[256,2048]{1,0:T(8,128)(2,1)S(1)} %get-tuple-element.142), channel_id=1, source_target_pairs={{0,1},{1,0},{2,3},{3,2},{4,5},{5,4},{6,7},{7,6},{8,9},{9,8},{10,11... | collective-permute-start | bytes 3145736 | tf_op jit(solution)/shard_map/ppermute | solution.py:517
  109.6 4.9 %collective-permute-start.34 = (bf16[64,2048]{1,0:T(8,128)(2,1)S(1)}, bf16[64,2048]{1,0:T(8,128)(2,1)S(1)}, u32[]{:S(2)}, u32[]{:S(2)}) collective-permute-start(bf16[64,2048]{1,0:T(8,128)(2,1)S(1)} %collective-permute-done.29.refs_0_), channel_id=1, source_target_pairs={{0,1},{1,0},{2,3},{3,2},{4,5},{5,4},{6,7},{7,6},{8,9},{9,8},{10,11... | collective-permute-start | bytes 786440 | tf_op jit(solution)/shard_map/ppermute | solution.py:517
  110.1 4.4 %collective-permute-start.35 = (bf16[64,2048]{1,0:T(8,128)(2,1)S(1)}, bf16[64,2048]{1,0:T(8,128)(2,1)S(1)}, u32[]{:S(2)}, u32[]{:S(2)}) collective-permute-start(bf16[64,2048]{1,0:T(8,128)(2,1)S(1)} %collective-permute-done.30.refs_1_), channel_id=1, source_target_pairs={{0,1},{1,0},{2,3},{3,2},{4,5},{5,4},{6,7},{7,6},{8,9},{9,8},{10,11... | collective-permute-start | bytes 786440 | tf_op jit(solution)/shard_map/ppermute | solution.py:517
  110.2 16.1 %collective-permute-start.44 = (bf16[256,2048]{1,0:T(8,128)(2,1)S(1)}, bf16[256,2048]{1,0:T(8,128)(2,1)S(1)}, u32[]{:S(2)}, u32[]{:S(2)}) collective-permute-start(bf16[256,2048]{1,0:T(8,128)(2,1)S(1)} %get-tuple-element.165), channel_id=1, source_target_pairs={{0,1},{1,0},{2,3},{3,2},{4,5},{5,4},{6,7},{7,6},{8,9},{9,8},{10,11... | collective-permute-start | bytes 3145736 | tf_op jit(solution)/shard_map/ppermute | solution.py:517
  112.4 8.4 %collective-permute-start.36 = (bf16[64,2048]{1,0:T(8,128)(2,1)S(1)}, bf16[64,2048]{1,0:T(8,128)(2,1)S(1)}, u32[]{:S(2)}, u32[]{:S(2)}) collective-permute-start(bf16[64,2048]{1,0:T(8,128)(2,1)S(1)} %add.23), channel_id=1, source_target_pairs={{4,0},{5,1},{8,4},{9,5},{12,8},{13,9},{14,12},{15,13},{10,14},{11,... | collective-permute-start | bytes 786440 | tf_op jit(solution)/shard_map/ppermute | solution.py:514
  113.9 8.1 %collective-permute-start.37 = (bf16[64,2048]{1,0:T(8,128)(2,1)S(1)}, bf16[64,2048]{1,0:T(8,128)(2,1)S(1)}, u32[]{:S(2)}, u32[]{:S(2)}) collective-permute-start(bf16[64,2048]{1,0:T(8,128)(2,1)S(1)} %add.24), channel_id=1, source_target_pairs={{0,4},{1,5},{4,8},{5,9},{8,12},{9,13},{12,14},{13,15},{14,10},{15,... | collective-permute-start | bytes 786440 | tf_op jit(solution)/shard_map/ppermute | solution.py:511
  122.1 1.9 %collective-permute-start.38 = (bf16[128,2048]{1,0:T(8,128)(2,1)S(1)}, bf16[128,2048]{1,0:T(8,128)(2,1)S(1)}, u32[]{:S(2)}, u32[]{:S(2)}) collective-permute-start(bf16[128,2048]{1,0:T(8,128)(2,1)S(1)} %get-tuple-element.153), channel_id=1, source_target_pairs={{0,1},{1,0},{2,3},{3,2},{4,5},{5,4},{6,7},{7,6},{8,9},{9,8},{10,11... | collective-permute-start | bytes 1572872 | tf_op jit(solution)/shard_map/ppermute | solution.py:517
  122.1 22.2 %collective-permute-start.43 = (bf16[256,2048]{1,0:T(8,128)(2,1)S(1)}, bf16[256,2048]{1,0:T(8,128)(2,1)S(1)}, u32[]{:S(2)}, u32[]{:S(2)}) collective-permute-start(bf16[256,2048]{1,0:T(8,128)(2,1)S(1)} %get-tuple-element.163), channel_id=1, source_target_pairs={{0,1},{1,0},{2,3},{3,2},{4,5},{5,4},{6,7},{7,6},{8,9},{9,8},{10,11... | collective-permute-start | bytes 3145736 | tf_op jit(solution)/shard_map/ppermute | solution.py:517
  124.0 9.2 %collective-permute-start.39 = (bf16[64,2048]{1,0:T(8,128)(2,1)S(1)}, bf16[64,2048]{1,0:T(8,128)(2,1)S(1)}, u32[]{:S(2)}, u32[]{:S(2)}) collective-permute-start(bf16[64,2048]{1,0:T(8,128)(2,1)S(1)} %add.25), channel_id=1, source_target_pairs={{4,0},{5,1},{8,4},{9,5},{12,8},{13,9},{14,12},{15,13},{10,14},{11,... | collective-permute-start | bytes 786440 | tf_op jit(solution)/shard_map/ppermute | solution.py:514
  125.6 9.2 %collective-permute-start.49 = (bf16[64,2048]{1,0:T(8,128)(2,1)S(1)}, bf16[64,2048]{1,0:T(8,128)(2,1)S(1)}, u32[]{:S(2)}, u32[]{:S(2)}) collective-permute-start(bf16[64,2048]{1,0:T(8,128)(2,1)S(1)} %add.31), channel_id=1, source_target_pairs={{0,4},{1,5},{4,8},{5,9},{8,12},{9,13},{12,14},{13,15},{14,10},{15,... | collective-permute-start | bytes 786440 | tf_op jit(solution)/shard_map/ppermute | solution.py:511
  126.2 28.9 %collective-permute-start.41 = (bf16[128,2048]{1,0:T(8,128)(2,1)S(1)}, bf16[128,2048]{1,0:T(8,128)(2,1)S(1)}, u32[]{:S(2)}, u32[]{:S(2)}) collective-permute-start(bf16[128,2048]{1,0:T(8,128)(2,1)S(1)} %get-tuple-element.160), channel_id=1, source_target_pairs={{0,1},{1,0},{2,3},{3,2},{4,5},{5,4},{6,7},{7,6},{8,9},{9,8},{10,11... | collective-permute-start | bytes 1572872 | tf_op jit(solution)/shard_map/ppermute | solution.py:517
  126.3 18.6 %collective-permute-start.45 = (bf16[64,2048]{1,0:T(8,128)(2,1)S(1)}, bf16[64,2048]{1,0:T(8,128)(2,1)S(1)}, u32[]{:S(2)}, u32[]{:S(2)}) collective-permute-start(bf16[64,2048]{1,0:T(8,128)(2,1)S(1)} %add.27), channel_id=1, source_target_pairs={{4,0},{5,1},{8,4},{9,5},{12,8},{13,9},{14,12},{15,13},{10,14},{11,... | collective-permute-start | bytes 786440 | tf_op jit(solution)/shard_map/ppermute | solution.py:514
  133.3 10.3 %collective-permute-start.40 = (bf16[64,2048]{1,0:T(8,128)(2,1)S(1)}, bf16[64,2048]{1,0:T(8,128)(2,1)S(1)}, u32[]{:S(2)}, u32[]{:S(2)}) collective-permute-start(bf16[64,2048]{1,0:T(8,128)(2,1)S(1)} %add.26), channel_id=1, source_target_pairs={{4,0},{5,1},{8,4},{9,5},{12,8},{13,9},{14,12},{15,13},{10,14},{11,... | collective-permute-start | bytes 786440 | tf_op jit(solution)/shard_map/ppermute | solution.py:514
  134.9 6.8 %collective-permute-start.50 = (bf16[64,2048]{1,0:T(8,128)(2,1)S(1)}, bf16[64,2048]{1,0:T(8,128)(2,1)S(1)}, u32[]{:S(2)}, u32[]{:S(2)}) collective-permute-start(bf16[64,2048]{1,0:T(8,128)(2,1)S(1)} %add.32), channel_id=1, source_target_pairs={{0,4},{1,5},{4,8},{5,9},{8,12},{9,13},{12,14},{13,15},{14,10},{15,... | collective-permute-start | bytes 786440 | tf_op jit(solution)/shard_map/ppermute | solution.py:511
  141.7 8.9 %collective-permute-start.53 = (bf16[64,2048]{1,0:T(8,128)(2,1)S(1)}, bf16[64,2048]{1,0:T(8,128)(2,1)S(1)}, u32[]{:S(2)}, u32[]{:S(2)}) collective-permute-start(bf16[64,2048]{1,0:T(8,128)(2,1)S(1)} %add.35), channel_id=1, source_target_pairs={{0,4},{1,5},{4,8},{5,9},{8,12},{9,13},{12,14},{13,15},{14,10},{15,... | collective-permute-start | bytes 786440 | tf_op jit(solution)/shard_map/ppermute | solution.py:511
  143.7 10.0 %collective-permute-start.51 = (bf16[64,2048]{1,0:T(8,128)(2,1)S(1)}, bf16[64,2048]{1,0:T(8,128)(2,1)S(1)}, u32[]{:S(2)}, u32[]{:S(2)}) collective-permute-start(bf16[64,2048]{1,0:T(8,128)(2,1)S(1)} %add.33), channel_id=1, source_target_pairs={{0,4},{1,5},{4,8},{5,9},{8,12},{9,13},{12,14},{13,15},{14,10},{15,... | collective-permute-start | bytes 786440 | tf_op jit(solution)/shard_map/ppermute | solution.py:511
  144.2 12.9 %collective-permute-start.42 = (bf16[128,2048]{1,0:T(8,128)(2,1)S(1)}, bf16[128,2048]{1,0:T(8,128)(2,1)S(1)}, u32[]{:S(2)}, u32[]{:S(2)}) collective-permute-start(bf16[128,2048]{1,0:T(8,128)(2,1)S(1)} %get-tuple-element.161), channel_id=1, source_target_pairs={{0,16},{1,17},{2,18},{3,19},{4,20},{5,21},{6,22},{7,23},{8,24},{9,... | collective-permute-start | bytes 1572872 | tf_op jit(solution)/shard_map/ppermute | solution.py:525
  144.9 9.5 %collective-permute-start.47 = (bf16[64,2048]{1,0:T(8,128)(2,1)S(1)}, bf16[64,2048]{1,0:T(8,128)(2,1)S(1)}, u32[]{:S(2)}, u32[]{:S(2)}) collective-permute-start(bf16[64,2048]{1,0:T(8,128)(2,1)S(1)} %add.29), channel_id=1, source_target_pairs={{4,0},{5,1},{8,4},{9,5},{12,8},{13,9},{14,12},{15,13},{10,14},{11,... | collective-permute-start | bytes 786440 | tf_op jit(solution)/shard_map/ppermute | solution.py:514
  150.6 9.2 %collective-permute-start.46 = (bf16[64,2048]{1,0:T(8,128)(2,1)S(1)}, bf16[64,2048]{1,0:T(8,128)(2,1)S(1)}, u32[]{:S(2)}, u32[]{:S(2)}) collective-permute-start(bf16[64,2048]{1,0:T(8,128)(2,1)S(1)} %add.28), channel_id=1, source_target_pairs={{4,0},{5,1},{8,4},{9,5},{12,8},{13,9},{14,12},{15,13},{10,14},{11,... | collective-permute-start | bytes 786440 | tf_op jit(solution)/shard_map/ppermute | solution.py:514
  153.7 8.6 %collective-permute-start.54 = (bf16[64,2048]{1,0:T(8,128)(2,1)S(1)}, bf16[64,2048]{1,0:T(8,128)(2,1)S(1)}, u32[]{:S(2)}, u32[]{:S(2)}) collective-permute-start(bf16[64,2048]{1,0:T(8,128)(2,1)S(1)} %add.36), channel_id=1, source_target_pairs={{0,4},{1,5},{4,8},{5,9},{8,12},{9,13},{12,14},{13,15},{14,10},{15,... | collective-permute-start | bytes 786440 | tf_op jit(solution)/shard_map/ppermute | solution.py:511
  154.4 10.7 %collective-permute-start.52 = (bf16[64,2048]{1,0:T(8,128)(2,1)S(1)}, bf16[64,2048]{1,0:T(8,128)(2,1)S(1)}, u32[]{:S(2)}, u32[]{:S(2)}) collective-permute-start(bf16[64,2048]{1,0:T(8,128)(2,1)S(1)} %add.34), channel_id=1, source_target_pairs={{0,4},{1,5},{4,8},{5,9},{8,12},{9,13},{12,14},{13,15},{14,10},{15,... | collective-permute-start | bytes 786440 | tf_op jit(solution)/shard_map/ppermute | solution.py:511
  155.1 10.0 %collective-permute-start.48 = (bf16[64,2048]{1,0:T(8,128)(2,1)S(1)}, bf16[64,2048]{1,0:T(8,128)(2,1)S(1)}, u32[]{:S(2)}, u32[]{:S(2)}) collective-permute-start(bf16[64,2048]{1,0:T(8,128)(2,1)S(1)} %add.30), channel_id=1, source_target_pairs={{4,0},{5,1},{8,4},{9,5},{12,8},{13,9},{14,12},{15,13},{10,14},{11,... | collective-permute-start | bytes 786440 | tf_op jit(solution)/shard_map/ppermute | solution.py:514
where the time goes:
time: 166 us
  waiting for transfers between devices  72.2 us (43%)
  Pallas kernels  49.6 us (30%)
  starting transfers between devices  42.8 us (26%)
    ppermute x16, waiting for transfers between devices, to_behind(): return lax.ppermute(x, 'exp', behind)  37.3 us
    pallas_call x5, Pallas kernels, expert(): pl.pallas_call(functools.partial(expert_kernel, first, blocks, len(inputs...  30 us
    ppermute x16, waiting for transfers between devices, to_ahead(): return lax.ppermute(x, 'exp', ahead)  24.4 us
    ppermute x16, starting transfers between devices, to_behind(): return lax.ppermute(x, 'exp', behind)  23.5 us
    ppermute x16, starting transfers between devices, to_ahead(): return lax.ppermute(x, 'exp', ahead)  8.57 us
    ppermute x5, starting transfers between devices, to_request(): return lax.ppermute(x, ('req', 'exp'), pairs)  6.43 us
    ppermute x18, waiting for transfers between devices, to_core(): return lax.ppermute(x, 'exp', [(d, d ^ 1) for d in range(exp_size)])  5.43 us
    ppermute x5, waiting for transfers between devices, to_request(): return lax.ppermute(x, ('req', 'exp'), pairs)  5.12 us
  transfers between devices with their start and end apart: 55, of which 30 were waited for; matrix products, arithmetic and copies ran while one was open for 0% of the time, Pallas kernels for 25%

commit v1 on v0

--- a/solution.py
+++ b/solution.py
@@ -107,18 +107,6 @@
     )(*operands)
 
 
-def join_kernel(where_ref, mine_ref, other_ref, out_ref):
-    rows = mine_ref.shape[0]
-    core = where_ref[1]
-    out_ref[pl.ds(pl.multiple_of(core * rows, 16), rows)] = mine_ref[...]
-    out_ref[pl.ds(pl.multiple_of((1 - core) * rows, 16), rows)] = other_ref[...]
-
-
-def join(where, mine, other):
-    shape = jax.ShapeDtypeStruct((2 * mine.shape[0], mine.shape[1]), mine.dtype)
-    return small_call(join_kernel, "join", [shape], [where, mine, other], 8 * mine.size)[0]
-
-
 def pack_kernel(count, part, where_ref, attn_hbm, residual_hbm, *refs):
     width = attn_hbm.shape[1]
     outs, sems = refs[:-1], refs[-1]
@@ -193,17 +181,15 @@
     at = visits
     chips = ring_ref.shape[0] // 2
     position = ring_ref[where_ref[0] // 2]
-    for offset, pieces in blocks:
+    first_core = where_ref[1] == 0
+    for offset in blocks:
         chip = ring_ref[chips + lax.rem(position + offset + chips, chips)]
         start = pl.multiple_of(chip * 2 * wrows, 128)
         columns = jnp.concatenate([r[:, pl.ds(start, 2 * wrows)] for r in rows_refs], axis=0)
-        step = wrows + TABLE_ROWS
-        if pieces == 1:
-            parts = [refs[at][i * step : i * step + wrows] for i in range(2)]
-        else:
-            parts = [refs[at + i][:wrows] for i in range(2)]
-        at += pieces
-        term = mm(columns, jnp.concatenate(parts, axis=0))
+        mine, other = refs[at][:wrows], refs[at + 1][:wrows]
+        at += 2
+        weight = jnp.concatenate([jnp.where(first_core, mine, other), jnp.where(first_core, other, mine)], axis=0)
+        term = mm(columns, weight)
         total = term if total is None else total + term
     if final:
         total = total + refs[at][...]
@@ -240,28 +226,19 @@
     )(*operands)
 
 
-def tables_kernel(wrows, slots, topk, rows, pieces, where_ref, *refs):
+def tables_kernel(wrows, slots, topk, rows, where_ref, *refs):
     pick_ref, put_ref, factor_ref = refs[-3:]
     both = 2 * rows
     expert_id = where_ref[0].astype(F32)
-    first_core = where_ref[1] == 0
     row_of = lax.broadcasted_iota(jnp.int32, (both, both), 0)
     row_at = lax.broadcasted_iota(jnp.int32, (both, both), 1)
     slot_of = lax.broadcasted_iota(jnp.int32, (slots, both), 0).astype(F32)
     slot_at = lax.broadcasted_iota(jnp.int32, (both, slots), 1).astype(F32)
-    step = wrows + TABLE_ROWS
-    at = 0
     for block in range(pick_ref.shape[0]):
-        if pieces[block] == 1:
-            named = [refs[at][i * step + wrows : (i + 1) * step] for i in range(2)]
-        else:
-            named = [refs[at + i][wrows:] for i in range(2)]
-        at += pieces[block]
-        named = [n.astype(F32) for n in named]
-        ordered = [jnp.where(first_core, named[0], named[1]), jnp.where(first_core, named[1], named[0])]
+        named = [refs[2 * block + i][wrows:].astype(F32) for i in range(2)]
         per_row = named[0].shape[1] // rows
         selected, factor = [], []
-        for n in ordered:
+        for n in named:
             item = [n[i // per_row : i // per_row + 1, (i % per_row) * rows : (i % per_row + 1) * rows] for i in range(4 * topk)]
             hits = [item[k] == expert_id for k in range(topk)]
             values = [item[topk + k] + item[2 * topk + k] + item[3 * topk + k] for k in range(topk)]
@@ -280,11 +257,11 @@
         factor_ref[block] = jnp.sum(jnp.where(taken, factor, 0.0), axis=1, keepdims=True)
 
 
-def tables(wrows, slots, topk, rows, where, pieces, blocks):
-    chips = len(pieces)
+def tables(wrows, slots, topk, rows, where, blocks):
+    chips = len(blocks) // 2
     both = 2 * rows
     return pl.pallas_call(
-        functools.partial(tables_kernel, wrows, slots, topk, rows, pieces),
+        functools.partial(tables_kernel, wrows, slots, topk, rows),
         out_shape=[
             jax.ShapeDtypeStruct((chips, slots, both), BF16),
             jax.ShapeDtypeStruct((chips, both, slots), BF16),
@@ -525,31 +502,30 @@
         return lax.ppermute(x, ("req", "exp"), pairs)
 
     weight_own, weight_sent = prepare(part, here, expert_ids.T, gate_weights.T, out_weight)
-    weight = join(here, weight_own, to_core(weight_sent))
-    low = high = weight
-    pairs = []
+    weight_met = to_core(weight_sent)
+    chains = [(weight_own, weight_own), (weight_met, weight_met)]
+    arrived = [[weight_own, weight_met]]
     for _ in range(1, depth):
-        low, high = to_ahead(low), to_behind(high)
-        pairs.append((low, high))
-    cut = wrows + TABLE_ROWS
-    last = [to_ahead(low[:cut]), to_behind(high[cut:])]
-
-    weight, attn_out, residual = lax.optimization_barrier((weight, attn_out, residual))
+        chains = [(to_ahead(low), to_behind(high)) for low, high in chains]
+        (low_own, high_own), (low_met, high_met) = chains
+        arrived += [[low_own, low_met], [high_own, high_met]]
+
+    weight_met, attn_out, residual = lax.optimization_barrier((weight_met, attn_out, residual))
     packed = pack(req_size, part, here, attn_out, residual)
     visits = [packed[0]] + [to_request(packed[shift], shift) for shift in range(1, req_size)]
-    passed = min(1, depth - 2)
-    pairs[passed], visits[1:] = lax.optimization_barrier((pairs[passed], visits[1:]))
+    arrived[-2:], visits[1:] = lax.optimization_barrier((arrived[-2:], visits[1:]))
     visits += [to_core(v) for v in visits]
-
-    early = [weight] + [w for pair in pairs[:-1] for w in pair]
-    late = last + list(pairs[-1])
-    tabs_early = tables(wrows, slots, topk, rows, here, [1] * (chips - 3), early)
-    whole = early + list(pairs[-1])
-    places = [(0, 1)] + [(side * k, 1) for k in range(1, depth) for side in (-1, 1)]
+    last = [to_ahead(arrived[-2][0]), to_behind(arrived[-1][1])]
+
+    early = [w for block in arrived[:-2] for w in block]
+    late = last + [w for block in arrived[-2:] for w in block]
+    tabs_early = tables(wrows, slots, topk, rows, here, early)
+    whole = [w for block in arrived for w in block]
+    places = [0] + [side * k for k in range(1, depth) for side in (-1, 1)]
     (acc,) = proj(wrows, places, here, ring, visits, whole)
     acc, tabs_early = lax.optimization_barrier((acc, tabs_early))
-    product = proj(wrows, [(depth, 2)], here, ring, visits, last, acc)
-    tabs_late = tables(wrows, slots, topk, rows, here, [2, 1, 1], late)
+    product = proj(wrows, [depth], here, ring, visits, last, acc)
+    tabs_late = tables(wrows, slots, topk, rows, here, late)
 
     got = {}
     for shift in reversed(range(req_size)):

time: 166 us -> 162 us (0.976)
  waiting for transfers between devices: 72.2 us -> 61.8 us
  starting transfers between devices: 42.8 us -> 49.6 us
    ppermute x16 -> x19, waiting for transfers between devices: 37.3 us -> 27.6 us  [to_behind(): return lax.ppermute(x, 'exp', behind)]
    ppermute x16 -> x19, starting transfers between devices: 23.5 us -> 29.6 us  [to_behind(): return lax.ppermute(x, 'exp', behind)]
    ppermute x16 -> x19, starting transfers between devices: 8.57 us -> 9.58 us  [to_ahead(): return lax.ppermute(x, 'exp', ahead)]
    pallas_call x6 -> x5, Pallas kernels: 3.43 us -> 2.86 us  [small_call(): pl.pallas_call(kernel, out_shape=shapes, in_specs=[smem()] + [vmem()] * (...]
    ppermute x16 -> x19, waiting for transfers between devices: 24.4 us -> 24.5 us  [to_ahead(): return lax.ppermute(x, 'exp', ahead)]
  transfers between devices with their start and end apart: 55 -> 61, of which waited for: 30 -> 35; matrix products, arithmetic and copies ran while one was open for 0% -> 0% of each run, Pallas kernels for 25% -> 26%
where the time goes in v1:
time: 162 us
  waiting for transfers between devices  61.8 us (38%)
  starting transfers between devices  49.6 us (31%)
  Pallas kernels  49.3 us (30%)
    pallas_call x5, Pallas kernels, expert(): pl.pallas_call(functools.partial(expert_kernel, first, blocks, len(inputs...  30 us
    ppermute x19, starting transfers between devices, to_behind(): return lax.ppermute(x, 'exp', behind)  29.6 us
    ppermute x19, waiting for transfers between devices, to_behind(): return lax.ppermute(x, 'exp', behind)  27.6 us
    ppermute x19, waiting for transfers between devices, to_ahead(): return lax.ppermute(x, 'exp', ahead)  24.5 us
    ppermute x19, starting transfers between devices, to_ahead(): return lax.ppermute(x, 'exp', ahead)  9.58 us
    ppermute x5, starting transfers between devices, to_request(): return lax.ppermute(x, ('req', 'exp'), pairs)  5.88 us
    ppermute x18, waiting for transfers between devices, to_core(): return lax.ppermute(x, 'exp', [(d, d ^ 1) for d in range(exp_size)])  5.43 us
    pallas_call x1, Pallas kernels, shared_expert(): pl.pallas_call(functools.partial(shared_kernel, count), out_shape=shapes,...  4.82 us
  transfers between devices with their start and end apart: 61, of which 35 were waited for; matrix products, arithmetic and copies ran while one was open for 0% of the time, Pallas kernels for 26%

profile of v1, /device:TPU:0, one launch (start us, length us, event | category | flops | bytes accessed | tf_op | source)
XLA Modules:
  0.0 161.9 jit_solution(5407579712723108699)
XLA Ops:
  0.1 1.8 %prepare.1 = (bf16[144,512]{1,0:T(8,128)(2,1)S(1)}, bf16[144,512]{1,0:T(8,128)(2,1)S(1)}) custom-call(s32[3]{0:T(128)S(1)} %pad_add_fusion.where_ref, s32[6,128]{1,0:T(8,128)} %bitcast.37, f32[6,128]{1,0:T(8,128)} %bitcast.38, bf16[128,2048]{1,0:T(8,128)(2,1)} %weight_hbm.1), custom_call_target="tpu_custom_call" | custom-call | bytes 524288 | tf_op jit(solution)/shard_map/prepare/pallas_call | solution.py:82
  2.4 1.0 collective-permute-done.refs_5_.refs_1_
  3.4 2.2 %pack.1 = (bf16[128,3072]{1,0:T(8,128)(2,1)S(1)}, bf16[128,3072]{1,0:T(8,128)(2,1)S(1)}) custom-call(s32[3]{0:T(128)S(1)} %pad_add_fusion.where_ref, bf16[128,2048]{1,0:T(8,128)(2,1)} %attn_hbm, bf16[128,2048]{1,0:T(8,128)(2,1)} %residual_hbm), custom_call_target="tpu_custom_call" | custom-call | bytes 2097152 | tf_op jit(solution)/shard_map/pack/pallas_call | solution.py:132
  5.6 2.9 %collective-permute-start.13 = (bf16[128,3072]{1,0:T(8,128)(2,1)S(1)}, bf16[128,3072]{1,0:T(8,128)(2,1)S(1)}, u32[]{:S(2)}, u32[]{:S(2)}) collective-permute-start(bf16[128,3072]{1,0:T(8,128)(2,1)S(1)} %get-tuple-element.94), channel_id=1, source_target_pairs={{0,16},{1,17},{2,18},{3,19},{4,20},{5,21},{6,22},{7,23},{8,24},{9,... | collective-permute-start | bytes 2359304 | tf_op jit(solution)/shard_map/ppermute | solution.py:502
  8.6 1.5 collective-permute-start.7
  10.6 1.5 collective-permute-start.10
  12.6 2.7 %collective-permute-done.7.refs_8_.refs_4_ = bf16[144,512]{1,0:T(8,128)(2,1)S(1)} collective-permute-done((bf16[144,512]{1,0:T(8,128)(2,1)S(1)}, bf16[144,512]{1,0:T(8,128)(2,1)S(1)}, u32[]{:S(2)}, u32[]{:S(2)}) %collective-permute-start.7) | collective-permute-done | bytes 147488 | tf_op jit(solution)/shard_map/ppermute | solution.py:491
  15.3 1.5 collective-permute-start.8
  17.4 1.1 collective-permute-done.10.refs_9_.refs_5_
  18.4 1.5 collective-permute-start.11
  20.5 1.5 collective-permute-done.8.refs_12_.refs_8_
  22.1 1.5 collective-permute-start.9
  24.1 1.1 collective-permute-done.11.refs_13_.refs_9_
  25.2 1.5 collective-permute-start.12
  27.3 1.1 collective-permute-done.9.refs_16_.refs_4_
  28.4 1.2 collective-permute-done.3.refs_14_.refs_2_
  30.4 1.6 collective-permute-done.6.refs_15_.refs_3_
  31.9 1.5 tables.2
  34.0 1.5 collective-permute-start.17
  36.2 1.7 %proj_part.1.refs_6_ = f32[512,512]{1,0:T(8,128)S(1)} custom-call(s32[3]{0:T(128)S(1)} %pad_add_fusion.where_ref, s32[16]{0:T(128)S(1)} %copy-done.2, bf16[128,3072]{1,0:T(8,128)(2,1)S(1)} %get-tuple-element.92.refs_0_, bf16[128,3072]{1,0:T(8,128)(2,1)S(1)} %collective-permute-done.13.refs_1_, bf16[128,3072]{1,0:T(8,128)(2,1)S(1)} %collective-permute-done.14.refs_2_, ...), custom_call_target="tpu_custom_call" | custom-call | flops 1879048192 | bytes 3932160 | tf_op jit(solution)/shard_map/proj_part/pallas_call | solution.py:214
  37.9 1.9 %collective-permute-done.16.refs_4_.refs_0_ = bf16[144,512]{1,0:T(8,128)(2,1)S(1)} collective-permute-done((bf16[144,512]{1,0:T(8,128)(2,1)S(1)}, bf16[144,512]{1,0:T(8,128)(2,1)S(1)}, u32[]{:S(2)}, u32[]{:S(2)}) %collective-permute-start.16) | collective-permute-done | bytes 147488 | tf_op jit(solution)/shard_map/ppermute | solution.py:488
  40.0 0.9 proj_final.1
  40.9 1.3 collective-permute-done.18.refs_1_
  42.8 1.6 collective-permute-start.20
  45.9 1.1 tables.3
  47.0 4.3 %collective-permute-done.21.refs_0_ = bf16[128,512]{1,0:T(8,128)(2,1)S(1)} collective-permute-done((bf16[128,512]{1,0:T(8,128)(2,1)S(1)}, bf16[128,512]{1,0:T(8,128)(2,1)S(1)}, u32[]{:S(2)}, u32[]{:S(2)}) %collective-permute-start.21) | collective-permute-done | bytes 131104 | tf_op jit(solution)/shard_map/ppermute | solution.py:502
  53.1 0.8 collective-permute-start.25
  53.9 1.6 collective-permute-start.24
  56.0 4.2 %expert.5 = (bf16[128,2048]{1,0:T(8,128)(2,1)S(1)}, bf16[128,2048]{1,0:T(8,128)(2,1)S(1)}) custom-call(f32[1,2048]{1,0:T(1,128)S(1)} %bitcast.31, bf16[5,144,256]{2,1,0:T(8,128)(2,1)S(1)} %get-tuple-element.116.pick_ref, bf16[5,256,144]{2,1,0:T(8,128)(2,1)S(1)} %get-tuple-element.117.put_ref, f32[5,144,1]{2,1,0:T(8,128)S(1)} %get-tuple-element.118.factor_ref, ...), custom_call_target="tpu_custom_call" | custom-call | flops 4982833152 | bytes 4194304 | tf_op jit(solution)/shard_map/expert/pallas_call | solution.py:315
  60.2 2.0 %collective-permute-done.24.refs_1_ = bf16[128,1024]{1,0:T(8,128)(2,1)S(1)} collective-permute-done((bf16[128,1024]{1,0:T(8,128)(2,1)S(1)}, bf16[128,1024]{1,0:T(8,128)(2,1)S(1)}, u32[]{:S(2)}, u32[]{:S(2)}) %collective-permute-start.24) | collective-permute-done | bytes 262176 | tf_op jit(solution)/shard_map/ppermute | solution.py:491
  62.1 1.3 collective-permute-done.23.refs_1_
  65.3 1.6 collective-permute-start.27
  67.3 7.2 %expert.6 = (bf16[128,2048]{1,0:T(8,128)(2,1)S(1)}, bf16[128,2048]{1,0:T(8,128)(2,1)S(1)}, bf16[256,2048]{1,0:T(8,128)(2,1)S(1)}) custom-call(f32[1,2048]{1,0:T(1,128)S(1)} %bitcast.32, bf16[5,144,256]{2,1,0:T(8,128)(2,1)S(1)} %get-tuple-element.116.pick_ref, bf16[5,256,144]{2,1,0:T(8,128)(2,1)S(1)} %get-tuple-element.117.put_ref, ...), custom_call_target="tpu_custom_call" | custom-call | flops 9965666304 | bytes 8388608 | tf_op jit(solution)/shard_map/expert/pallas_call | solution.py:315
  74.5 4.6 %collective-permute-done.27.refs_2_ = bf16[128,2048]{1,0:T(8,128)(2,1)S(1)} collective-permute-done((bf16[128,2048]{1,0:T(8,128)(2,1)S(1)}, bf16[128,2048]{1,0:T(8,128)(2,1)S(1)}, u32[]{:S(2)}, u32[]{:S(2)}) %collective-permute-start.27) | collective-permute-done | bytes 524320 | tf_op jit(solution)/shard_map/ppermute | solution.py:491
  79.1 1.3 collective-permute-done.26.refs_0_
  81.9 1.6 collective-permute-start.31
  83.5 7.2 %expert.7 = (bf16[128,2048]{1,0:T(8,128)(2,1)S(1)}, bf16[128,2048]{1,0:T(8,128)(2,1)S(1)}, bf16[256,2048]{1,0:T(8,128)(2,1)S(1)}) custom-call(f32[1,2048]{1,0:T(1,128)S(1)} %bitcast.33, bf16[5,144,256]{2,1,0:T(8,128)(2,1)S(1)} %get-tuple-element.116.pick_ref, bf16[5,256,144]{2,1,0:T(8,128)(2,1)S(1)} %get-tuple-element.117.put_ref, ...), custom_call_target="tpu_custom_call" | custom-call | flops 9965666304 | bytes 8388608 | tf_op jit(solution)/shard_map/expert/pallas_call | solution.py:315
  90.7 4.3 %collective-permute-done.30.refs_0_ = bf16[128,2048]{1,0:T(8,128)(2,1)S(1)} collective-permute-done((bf16[128,2048]{1,0:T(8,128)(2,1)S(1)}, bf16[128,2048]{1,0:T(8,128)(2,1)S(1)}, u32[]{:S(2)}, u32[]{:S(2)}) %collective-permute-start.30) | collective-permute-done | bytes 524320 | tf_op jit(solution)/shard_map/ppermute | solution.py:488
  95.8 1.6 %collective-permute-start.36 = (bf16[64,2048]{1,0:T(8,128)(2,1)S(1)}, bf16[64,2048]{1,0:T(8,128)(2,1)S(1)}, u32[]{:S(2)}, u32[]{:S(2)}) collective-permute-start(bf16[64,2048]{1,0:T(8,128)(2,1)S(1)} %slice.7), channel_id=1, source_target_pairs={{4,0},{5,1},{8,4},{9,5},{12,8},{13,9},{14,12},{15,13},{10,14},{11,... | collective-permute-start | bytes 786440 | tf_op jit(solution)/shard_map/ppermute | solution.py:491
  97.9 7.2 %expert.8 = (bf16[128,2048]{1,0:T(8,128)(2,1)S(1)}, bf16[128,2048]{1,0:T(8,128)(2,1)S(1)}, bf16[256,2048]{1,0:T(8,128)(2,1)S(1)}) custom-call(f32[1,2048]{1,0:T(1,128)S(1)} %bitcast.34, bf16[3,144,256]{2,1,0:T(8,128)(2,1)S(1)} %get-tuple-element.137.pick_ref, bf16[3,256,144]{2,1,0:T(8,128)(2,1)S(1)} %get-tuple-element.138.put_ref, ...), custom_call_target="tpu_custom_call" | custom-call | flops 9965666304 | bytes 8388608 | tf_op jit(solution)/shard_map/expert/pallas_call | solution.py:315
  106.4 1.6 %collective-permute-done.39.refs_1_ = bf16[256,2048]{1,0:T(8,128)(2,1)S(1)} collective-permute-done((bf16[256,2048]{1,0:T(8,128)(2,1)S(1)}, bf16[256,2048]{1,0:T(8,128)(2,1)S(1)}, u32[]{:S(2)}, u32[]{:S(2)}) %collective-permute-start.39) | collective-permute-done | bytes 1048608 | tf_op jit(solution)/shard_map/ppermute | solution.py:494
  108.1 1.6 %collective-permute-start.42 = (bf16[64,2048]{1,0:T(8,128)(2,1)S(1)}, bf16[64,2048]{1,0:T(8,128)(2,1)S(1)}, u32[]{:S(2)}, u32[]{:S(2)}) collective-permute-start(bf16[64,2048]{1,0:T(8,128)(2,1)S(1)} %add.23), channel_id=1, source_target_pairs={{4,0},{5,1},{8,4},{9,5},{12,8},{13,9},{14,12},{15,13},{10,14},{11,... | collective-permute-start | bytes 786440 | tf_op jit(solution)/shard_map/ppermute | solution.py:491
  110.3 4.2 %expert.9 = (bf16[128,2048]{1,0:T(8,128)(2,1)S(1)}, bf16[128,2048]{1,0:T(8,128)(2,1)S(1)}) custom-call(f32[1,2048]{1,0:T(1,128)S(1)} %bitcast.35, bf16[3,144,256]{2,1,0:T(8,128)(2,1)S(1)} %get-tuple-element.137.pick_ref, bf16[3,256,144]{2,1,0:T(8,128)(2,1)S(1)} %get-tuple-element.138.put_ref, f32[3,144,1]{2,1,0:T(8,128)S(1)} %get-tuple-element.139.factor_ref, ...), custom_call_target="tpu_custom_call" | custom-call | flops 4982833152 | bytes 4194304 | tf_op jit(solution)/shard_map/expert/pallas_call | solution.py:315
  114.5 2.0 %collective-permute-done.42.refs_2_ = bf16[64,2048]{1,0:T(8,128)(2,1)S(1)} collective-permute-done((bf16[64,2048]{1,0:T(8,128)(2,1)S(1)}, bf16[64,2048]{1,0:T(8,128)(2,1)S(1)}, u32[]{:S(2)}, u32[]{:S(2)}) %collective-permute-start.42) | collective-permute-done | bytes 262176 | tf_op jit(solution)/shard_map/ppermute | solution.py:491
  116.5 1.4 collective-permute-done.43.refs_2_
  118.4 1.4 collective-permute-done.44.refs_1_
  119.9 1.6 collective-permute-start.45
  122.2 1.6 collective-permute-start.51
  123.8 5.3 %collective-permute-done.45.refs_2_ = bf16[64,2048]{1,0:T(8,128)(2,1)S(1)} collective-permute-done((bf16[64,2048]{1,0:T(8,128)(2,1)S(1)}, bf16[64,2048]{1,0:T(8,128)(2,1)S(1)}, u32[]{:S(2)}, u32[]{:S(2)}) %collective-permute-start.45) | collective-permute-done | bytes 262176 | tf_op jit(solution)/shard_map/ppermute | solution.py:491
  129.2 1.6 collective-permute-start.46
  130.9 0.8 collective-permute-start.56
  131.7 4.8 %shared.1 = (f32[128,2048]{1,0:T(8,128)S(1)}, bf16[128,2048]{1,0:T(8,128)(2,1)S(1)}) custom-call(f32[1,2048]{1,0:T(1,128)S(1)} %bitcast.36, bf16[704,2048]{1,0:T(8,128)(2,1)} %bitcast.39, bf16[704,2048]{1,0:T(8,128)(2,1)} %bitcast.40, bf16[704,2048]{1,0:T(8,128)(2,1)} %bitcast.41, bf16[128,2048]{1,0:T(8,128)(2,1)S(1)} %weave.3.refs_0_.refs_1_, ...), custom_call_target="tpu_custom_call" | custom-call | flops 4429185024 | bytes 10747904 | tf_op jit(solution)/shard_map/shared/pallas_call | solution.py:376
  136.6 1.1 collective-permute-done.56.refs_2_
  138.2 1.3 collective-permute-done.46.refs_2_
  139.9 1.5 collective-permute-start.48
  141.5 1.6 %collective-permute-start.53 = (bf16[64,2048]{1,0:T(8,128)(2,1)S(1)}, bf16[64,2048]{1,0:T(8,128)(2,1)S(1)}, u32[]{:S(2)}, u32[]{:S(2)}) collective-permute-start(bf16[64,2048]{1,0:T(8,128)(2,1)S(1)} %add.29), channel_id=1, source_target_pairs={{4,0},{5,1},{8,4},{9,5},{12,8},{13,9},{14,12},{15,13},{10,14},{11,... | collective-permute-start | bytes 786440 | tf_op jit(solution)/shard_map/ppermute | solution.py:491
  143.3 3.4 %collective-permute-done.59.refs_2_ = bf16[64,2048]{1,0:T(8,128)(2,1)S(1)} collective-permute-done((bf16[64,2048]{1,0:T(8,128)(2,1)S(1)}, bf16[64,2048]{1,0:T(8,128)(2,1)S(1)}, u32[]{:S(2)}, u32[]{:S(2)}) %collective-permute-start.59) | collective-permute-done | bytes 262176 | tf_op jit(solution)/shard_map/ppermute | solution.py:488
  146.6 1.3 collective-permute-start.52
  148.1 1.6 collective-permute-done.57.refs_2_
  151.4 1.6 %collective-permute-start.54 = (bf16[64,2048]{1,0:T(8,128)(2,1)S(1)}, bf16[64,2048]{1,0:T(8,128)(2,1)S(1)}, u32[]{:S(2)}, u32[]{:S(2)}) collective-permute-start(bf16[64,2048]{1,0:T(8,128)(2,1)S(1)} %add.30), channel_id=1, source_target_pairs={{4,0},{5,1},{8,4},{9,5},{12,8},{13,9},{14,12},{15,13},{10,14},{11,... | collective-permute-start | bytes 786440 | tf_op jit(solution)/shard_map/ppermute | solution.py:491
  153.3 3.1 %collective-permute-done.52.refs_0_ = bf16[64,2048]{1,0:T(8,128)(2,1)S(1)} collective-permute-done((bf16[64,2048]{1,0:T(8,128)(2,1)S(1)}, bf16[64,2048]{1,0:T(8,128)(2,1)S(1)}, u32[]{:S(2)}, u32[]{:S(2)}) %collective-permute-start.52) | collective-permute-done | bytes 262176 | tf_op jit(solution)/shard_map/ppermute | solution.py:491
  156.5 1.7 %collective-permute-done.60.refs_3_ = bf16[64,2048]{1,0:T(8,128)(2,1)S(1)} collective-permute-done((bf16[64,2048]{1,0:T(8,128)(2,1)S(1)}, bf16[64,2048]{1,0:T(8,128)(2,1)S(1)}, u32[]{:S(2)}, u32[]{:S(2)}) %collective-permute-start.60) | collective-permute-done | bytes 262176 | tf_op jit(solution)/shard_map/ppermute | solution.py:488
  158.2 2.8 %collective-permute-done.58.refs_2_ = bf16[64,2048]{1,0:T(8,128)(2,1)S(1)} collective-permute-done((bf16[64,2048]{1,0:T(8,128)(2,1)S(1)}, bf16[64,2048]{1,0:T(8,128)(2,1)S(1)}, u32[]{:S(2)}, u32[]{:S(2)}) %collective-permute-start.58) | collective-permute-done | bytes 262176 | tf_op jit(solution)/shard_map/ppermute | solution.py:488
  161.0 1.0 final.1
  (110 shorter events, 22.0 us)
Async XLA Ops:
  0.1 55.8 %copy-start = (bf16[1,1408,2048]{2,1,0:T(8,128)(2,1)S(1)}, bf16[1,1408,2048]{2,1,0:T(8,128)(2,1)}, u32[]{:S(2)}) copy-start(bf16[1,1408,2048]{2,1,0:T(8,128)(2,1)} %param.21) | copy-start | bytes 17301508
  1.9 1.5 collective-permute-start
  3.4 52.5 %slice-start.2 = ((s8[5767168]{0:T(1024)(128)(4,1)}), s8[4194304]{0:T(1024)(128)(4,1)S(1)}, s32[]{:S(2)}) async-start(s8[5767168]{0:T(1024)(128)(4,1)} %bitcast.19), calls=%async_computation.2 | async-start | bytes 8388608
  5.6 26.3 %collective-permute-start.13 = (bf16[128,3072]{1,0:T(8,128)(2,1)S(1)}, bf16[128,3072]{1,0:T(8,128)(2,1)S(1)}, u32[]{:S(2)}, u32[]{:S(2)}) collective-permute-start(bf16[128,3072]{1,0:T(8,128)(2,1)S(1)} %get-tuple-element.94), channel_id=1, source_target_pairs={{0,16},{1,17},{2,18},{3,19},{4,20},{5,21},{6,22},{7,23},{8,24},{9,... | collective-permute-start | bytes 2359304 | tf_op jit(solution)/shard_map/ppermute | solution.py:502
  8.6 6.7 %collective-permute-start.7 = (bf16[144,512]{1,0:T(8,128)(2,1)S(1)}, bf16[144,512]{1,0:T(8,128)(2,1)S(1)}, u32[]{:S(2)}, u32[]{:S(2)}) collective-permute-start(bf16[144,512]{1,0:T(8,128)(2,1)S(1)} %get-tuple-element.93.refs_4_.refs_0_), channel_id=1, source_target_pairs={{4,0},{5,1},{8,4},{9,5},{12,8},{13,9},{14,12},{15,13},{10,14},{11,... | collective-permute-start | bytes 442376 | tf_op jit(solution)/shard_map/ppermute | solution.py:491
  10.1 6.8 %collective-permute-start.1 = (bf16[144,512]{1,0:T(8,128)(2,1)S(1)}, bf16[144,512]{1,0:T(8,128)(2,1)S(1)}, u32[]{:S(2)}, u32[]{:S(2)}) collective-permute-start(bf16[144,512]{1,0:T(8,128)(2,1)S(1)} %get-tuple-element.93.refs_4_.refs_0_), channel_id=1, source_target_pairs={{0,4},{1,5},{4,8},{5,9},{8,12},{9,13},{12,14},{13,15},{14,10},{15,... | collective-permute-start | bytes 442376 | tf_op jit(solution)/shard_map/ppermute | solution.py:488
  10.6 7.9 %collective-permute-start.10 = (bf16[144,512]{1,0:T(8,128)(2,1)S(1)}, bf16[144,512]{1,0:T(8,128)(2,1)S(1)}, u32[]{:S(2)}, u32[]{:S(2)}) collective-permute-start(bf16[144,512]{1,0:T(8,128)(2,1)S(1)} %collective-permute-done.refs_5_.refs_1_), channel_id=1, source_target_pairs={{4,0},{5,1},{8,4},{9,5},{12,8},{13,9},{14,12},{15,13},{10,14},{11,... | collective-permute-start | bytes 442376 | tf_op jit(solution)/shard_map/ppermute | solution.py:491
  12.1 7.9 %collective-permute-start.4 = (bf16[144,512]{1,0:T(8,128)(2,1)S(1)}, bf16[144,512]{1,0:T(8,128)(2,1)S(1)}, u32[]{:S(2)}, u32[]{:S(2)}) collective-permute-start(bf16[144,512]{1,0:T(8,128)(2,1)S(1)} %collective-permute-done.refs_5_.refs_1_), channel_id=1, source_target_pairs={{0,4},{1,5},{4,8},{5,9},{8,12},{9,13},{12,14},{13,15},{14,10},{15,... | collective-permute-start | bytes 442376 | tf_op jit(solution)/shard_map/ppermute | solution.py:488
  15.3 6.8 %collective-permute-start.8 = (bf16[144,512]{1,0:T(8,128)(2,1)S(1)}, bf16[144,512]{1,0:T(8,128)(2,1)S(1)}, u32[]{:S(2)}, u32[]{:S(2)}) collective-permute-start(bf16[144,512]{1,0:T(8,128)(2,1)S(1)} %collective-permute-done.7.refs_8_.refs_4_), channel_id=1, source_target_pairs={{4,0},{5,1},{8,4},{9,5},{12,8},{13,9},{14,12},{15,13},{10,14},{11,... | collective-permute-start | bytes 442376 | tf_op jit(solution)/shard_map/ppermute | solution.py:491
  16.8 6.7 %collective-permute-start.2 = (bf16[144,512]{1,0:T(8,128)(2,1)S(1)}, bf16[144,512]{1,0:T(8,128)(2,1)S(1)}, u32[]{:S(2)}, u32[]{:S(2)}) collective-permute-start(bf16[144,512]{1,0:T(8,128)(2,1)S(1)} %collective-permute-done.1.refs_6_.refs_2_), channel_id=1, source_target_pairs={{0,4},{1,5},{4,8},{5,9},{8,12},{9,13},{12,14},{13,15},{14,10},{15,... | collective-permute-start | bytes 442376 | tf_op jit(solution)/shard_map/ppermute | solution.py:488
  18.4 6.8 %collective-permute-start.11 = (bf16[144,512]{1,0:T(8,128)(2,1)S(1)}, bf16[144,512]{1,0:T(8,128)(2,1)S(1)}, u32[]{:S(2)}, u32[]{:S(2)}) collective-permute-start(bf16[144,512]{1,0:T(8,128)(2,1)S(1)} %collective-permute-done.10.refs_9_.refs_5_), channel_id=1, source_target_pairs={{4,0},{5,1},{8,4},{9,5},{12,8},{13,9},{14,12},{15,13},{10,14},{11,... | collective-permute-start | bytes 442376 | tf_op jit(solution)/shard_map/ppermute | solution.py:491
  20.0 6.8 %collective-permute-start.5 = (bf16[144,512]{1,0:T(8,128)(2,1)S(1)}, bf16[144,512]{1,0:T(8,128)(2,1)S(1)}, u32[]{:S(2)}, u32[]{:S(2)}) collective-permute-start(bf16[144,512]{1,0:T(8,128)(2,1)S(1)} %collective-permute-done.4.refs_7_.refs_3_), channel_id=1, source_target_pairs={{0,4},{1,5},{4,8},{5,9},{8,12},{9,13},{12,14},{13,15},{14,10},{15,... | collective-permute-start | bytes 442376 | tf_op jit(solution)/shard_map/ppermute | solution.py:488
  22.1 6.3 %collective-permute-start.9 = (bf16[144,512]{1,0:T(8,128)(2,1)S(1)}, bf16[144,512]{1,0:T(8,128)(2,1)S(1)}, u32[]{:S(2)}, u32[]{:S(2)}) collective-permute-start(bf16[144,512]{1,0:T(8,128)(2,1)S(1)} %collective-permute-done.8.refs_12_.refs_8_), channel_id=1, source_target_pairs={{4,0},{5,1},{8,4},{9,5},{12,8},{13,9},{14,12},{15,13},{10,14},{11,... | collective-permute-start | bytes 442376 | tf_op jit(solution)/shard_map/ppermute | solution.py:491
  23.6 6.1 %collective-permute-start.3 = (bf16[144,512]{1,0:T(8,128)(2,1)S(1)}, bf16[144,512]{1,0:T(8,128)(2,1)S(1)}, u32[]{:S(2)}, u32[]{:S(2)}) collective-permute-start(bf16[144,512]{1,0:T(8,128)(2,1)S(1)} %collective-permute-done.2.refs_10_.refs_6_), channel_id=1, source_target_pairs={{0,4},{1,5},{4,8},{5,9},{8,12},{9,13},{12,14},{13,15},{14,10},{15,... | collective-permute-start | bytes 442376 | tf_op jit(solution)/shard_map/ppermute | solution.py:488
  25.2 5.1 %collective-permute-start.12 = (bf16[144,512]{1,0:T(8,128)(2,1)S(1)}, bf16[144,512]{1,0:T(8,128)(2,1)S(1)}, u32[]{:S(2)}, u32[]{:S(2)}) collective-permute-start(bf16[144,512]{1,0:T(8,128)(2,1)S(1)} %collective-permute-done.11.refs_13_.refs_9_), channel_id=1, source_target_pairs={{4,0},{5,1},{8,4},{9,5},{12,8},{13,9},{14,12},{15,13},{10,14},{11,... | collective-permute-start | bytes 442376 | tf_op jit(solution)/shard_map/ppermute | solution.py:491
  26.8 5.1 %collective-permute-start.6 = (bf16[144,512]{1,0:T(8,128)(2,1)S(1)}, bf16[144,512]{1,0:T(8,128)(2,1)S(1)}, u32[]{:S(2)}, u32[]{:S(2)}) collective-permute-start(bf16[144,512]{1,0:T(8,128)(2,1)S(1)} %collective-permute-done.5.refs_11_.refs_7_), channel_id=1, source_target_pairs={{0,4},{1,5},{4,8},{5,9},{8,12},{9,13},{12,14},{13,15},{14,10},{15,... | collective-permute-start | bytes 442376 | tf_op jit(solution)/shard_map/ppermute | solution.py:488
  28.4 7.2 %collective-permute-start.14 = (bf16[128,3072]{1,0:T(8,128)(2,1)S(1)}, bf16[128,3072]{1,0:T(8,128)(2,1)S(1)}, u32[]{:S(2)}, u32[]{:S(2)}) collective-permute-start(bf16[128,3072]{1,0:T(8,128)(2,1)S(1)} %get-tuple-element.92.refs_0_), channel_id=1, source_target_pairs={{0,1},{1,0},{2,3},{3,2},{4,5},{5,4},{6,7},{7,6},{8,9},{9,8},{10,11... | collective-permute-start | bytes 2359304 | tf_op jit(solution)/shard_map/ppermute | solution.py:494
  31.9 3.6 %collective-permute-start.15 = (bf16[128,3072]{1,0:T(8,128)(2,1)S(1)}, bf16[128,3072]{1,0:T(8,128)(2,1)S(1)}, u32[]{:S(2)}, u32[]{:S(2)}) collective-permute-start(bf16[128,3072]{1,0:T(8,128)(2,1)S(1)} %collective-permute-done.13.refs_1_), channel_id=1, source_target_pairs={{0,1},{1,0},{2,3},{3,2},{4,5},{5,4},{6,7},{7,6},{8,9},{9,8},{10,11... | collective-permute-start | bytes 2359304 | tf_op jit(solution)/shard_map/ppermute | solution.py:494
  31.9 24.0 %slice-start = ((s8[5767168]{0:T(1024)(128)(4,1)}), s8[4194304]{0:T(1024)(128)(4,1)S(1)}, s32[]{:S(2)}) async-start(s8[5767168]{0:T(1024)(128)(4,1)} %bitcast.12), calls=%async_computation | async-start | bytes 8388608
  33.5 6.3 %collective-permute-start.16 = (bf16[144,512]{1,0:T(8,128)(2,1)S(1)}, bf16[144,512]{1,0:T(8,128)(2,1)S(1)}, u32[]{:S(2)}, u32[]{:S(2)}) collective-permute-start(bf16[144,512]{1,0:T(8,128)(2,1)S(1)} %collective-permute-done.3.refs_14_.refs_2_), channel_id=1, source_target_pairs={{0,4},{1,5},{4,8},{5,9},{8,12},{9,13},{12,14},{13,15},{14,10},{15,... | collective-permute-start | bytes 442376 | tf_op jit(solution)/shard_map/ppermute | solution.py:488
  34.0 6.0 %collective-permute-start.17 = (bf16[144,512]{1,0:T(8,128)(2,1)S(1)}, bf16[144,512]{1,0:T(8,128)(2,1)S(1)}, u32[]{:S(2)}, u32[]{:S(2)}) collective-permute-start(bf16[144,512]{1,0:T(8,128)(2,1)S(1)} %collective-permute-done.12.refs_17_.refs_5_), channel_id=1, source_target_pairs={{4,0},{5,1},{8,4},{9,5},{12,8},{13,9},{14,12},{15,13},{10,14},{11,... | collective-permute-start | bytes 442376 | tf_op jit(solution)/shard_map/ppermute | solution.py:491
  40.9 1.4 collective-permute-start.18
  42.8 9.0 %collective-permute-start.20 = (bf16[128,1024]{1,0:T(8,128)(2,1)S(1)}, bf16[128,1024]{1,0:T(8,128)(2,1)S(1)}, u32[]{:S(2)}, u32[]{:S(2)}) collective-permute-start(bf16[128,1024]{1,0:T(8,128)(2,1)S(1)} %beside.2.refs_0_), channel_id=1, source_target_pairs={{4,0},{5,1},{8,4},{9,5},{12,8},{13,9},{14,12},{15,13},{10,14},{11,... | collective-permute-start | bytes 786440 | tf_op jit(solution)/shard_map/ppermute | solution.py:491
  44.4 8.1 %collective-permute-start.19 = (bf16[128,1024]{1,0:T(8,128)(2,1)S(1)}, bf16[128,1024]{1,0:T(8,128)(2,1)S(1)}, u32[]{:S(2)}, u32[]{:S(2)}) collective-permute-start(bf16[128,1024]{1,0:T(8,128)(2,1)S(1)} %beside.2.refs_0_), channel_id=1, source_target_pairs={{0,4},{1,5},{4,8},{5,9},{8,12},{9,13},{12,14},{13,15},{14,10},{15,... | collective-permute-start | bytes 786440 | tf_op jit(solution)/shard_map/ppermute | solution.py:488
  44.9 6.4 %collective-permute-start.21 = (bf16[128,512]{1,0:T(8,128)(2,1)S(1)}, bf16[128,512]{1,0:T(8,128)(2,1)S(1)}, u32[]{:S(2)}, u32[]{:S(2)}) collective-permute-start(bf16[128,512]{1,0:T(8,128)(2,1)S(1)} %get-tuple-element.106), channel_id=1, source_target_pairs={{0,16},{1,17},{2,18},{3,19},{4,20},{5,21},{6,22},{7,23},{8,24},{9,... | collective-permute-start | bytes 393224 | tf_op jit(solution)/shard_map/ppermute | solution.py:502
  45.3 6.0 %collective-permute-start.22 = (bf16[128,512]{1,0:T(8,128)(2,1)S(1)}, bf16[128,512]{1,0:T(8,128)(2,1)S(1)}, u32[]{:S(2)}, u32[]{:S(2)}) collective-permute-start(bf16[128,512]{1,0:T(8,128)(2,1)S(1)} %get-tuple-element.107), channel_id=1, source_target_pairs={{0,17},{1,16},{2,19},{3,18},{4,21},{5,20},{6,23},{7,22},{8,25},{9,... | collective-permute-start | bytes 393224 | tf_op jit(solution)/shard_map/ppermute | solution.py:502
  53.1 2.8 %collective-permute-start.25 = (bf16[128,2048]{1,0:T(8,128)(2,1)S(1)}, bf16[128,2048]{1,0:T(8,128)(2,1)S(1)}, u32[]{:S(2)}, u32[]{:S(2)}) collective-permute-start(bf16[128,2048]{1,0:T(8,128)(2,1)S(1)} %weave.3.refs_0_.refs_1_), channel_id=1, source_target_pairs={{0,1},{1,0},{2,3},{3,2},{4,5},{5,4},{6,7},{7,6},{8,9},{9,8},{10,11... | collective-permute-start | bytes 1572872 | tf_op jit(solution)/shard_map/ppermute | solution.py:494
  53.9 8.3 %collective-permute-start.24 = (bf16[128,1024]{1,0:T(8,128)(2,1)S(1)}, bf16[128,1024]{1,0:T(8,128)(2,1)S(1)}, u32[]{:S(2)}, u32[]{:S(2)}) collective-permute-start(bf16[128,1024]{1,0:T(8,128)(2,1)S(1)} %beside.3.refs_1_), channel_id=1, source_target_pairs={{4,0},{5,1},{8,4},{9,5},{12,8},{13,9},{14,12},{15,13},{10,14},{11,... | collective-permute-start | bytes 786440 | tf_op jit(solution)/shard_map/ppermute | solution.py:491
  55.4 8.0 %collective-permute-start.23 = (bf16[128,1024]{1,0:T(8,128)(2,1)S(1)}, bf16[128,1024]{1,0:T(8,128)(2,1)S(1)}, u32[]{:S(2)}, u32[]{:S(2)}) collective-permute-start(bf16[128,1024]{1,0:T(8,128)(2,1)S(1)} %beside.3.refs_1_), channel_id=1, source_target_pairs={{0,4},{1,5},{4,8},{5,9},{8,12},{9,13},{12,14},{13,15},{14,10},{15,... | collective-permute-start | bytes 786440 | tf_op jit(solution)/shard_map/ppermute | solution.py:488
  64.0 3.3 %collective-permute-start.29 = (bf16[128,2048]{1,0:T(8,128)(2,1)S(1)}, bf16[128,2048]{1,0:T(8,128)(2,1)S(1)}, u32[]{:S(2)}, u32[]{:S(2)}) collective-permute-start(bf16[128,2048]{1,0:T(8,128)(2,1)S(1)} %weave.5.refs_2_), channel_id=1, source_target_pairs={{0,1},{1,0},{2,3},{3,2},{4,5},{5,4},{6,7},{7,6},{8,9},{9,8},{10,11... | collective-permute-start | bytes 1572872 | tf_op jit(solution)/shard_map/ppermute | solution.py:494
  64.7 2.6 %collective-permute-start.28 = (bf16[128,2048]{1,0:T(8,128)(2,1)S(1)}, bf16[128,2048]{1,0:T(8,128)(2,1)S(1)}, u32[]{:S(2)}, u32[]{:S(2)}) collective-permute-start(bf16[128,2048]{1,0:T(8,128)(2,1)S(1)} %weave.4.refs_0_), channel_id=1, source_target_pairs={{0,1},{1,0},{2,3},{3,2},{4,5},{5,4},{6,7},{7,6},{8,9},{9,8},{10,11... | collective-permute-start | bytes 1572872 | tf_op jit(solution)/shard_map/ppermute | solution.py:494
  65.3 13.9 %collective-permute-start.27 = (bf16[128,2048]{1,0:T(8,128)(2,1)S(1)}, bf16[128,2048]{1,0:T(8,128)(2,1)S(1)}, u32[]{:S(2)}, u32[]{:S(2)}) collective-permute-start(bf16[128,2048]{1,0:T(8,128)(2,1)S(1)} %weave.5.refs_2_), channel_id=1, source_target_pairs={{4,0},{5,1},{8,4},{9,5},{12,8},{13,9},{14,12},{15,13},{10,14},{11,... | collective-permute-start | bytes 1572872 | tf_op jit(solution)/shard_map/ppermute | solution.py:491
  66.8 13.6 %collective-permute-start.26 = (bf16[128,2048]{1,0:T(8,128)(2,1)S(1)}, bf16[128,2048]{1,0:T(8,128)(2,1)S(1)}, u32[]{:S(2)}, u32[]{:S(2)}) collective-permute-start(bf16[128,2048]{1,0:T(8,128)(2,1)S(1)} %weave.4.refs_0_), channel_id=1, source_target_pairs={{0,4},{1,5},{4,8},{5,9},{8,12},{9,13},{12,14},{13,15},{14,10},{15,... | collective-permute-start | bytes 1572872 | tf_op jit(solution)/shard_map/ppermute | solution.py:488
  80.4 3.1 %collective-permute-start.32 = (bf16[128,2048]{1,0:T(8,128)(2,1)S(1)}, bf16[128,2048]{1,0:T(8,128)(2,1)S(1)}, u32[]{:S(2)}, u32[]{:S(2)}) collective-permute-start(bf16[128,2048]{1,0:T(8,128)(2,1)S(1)} %collective-permute-done.26.refs_0_), channel_id=1, source_target_pairs={{0,1},{1,0},{2,3},{3,2},{4,5},{5,4},{6,7},{7,6},{8,9},{9,8},{10,11... | collective-permute-start | bytes 1572872 | tf_op jit(solution)/shard_map/ppermute | solution.py:494
  80.4 3.1 %collective-permute-start.33 = (bf16[128,2048]{1,0:T(8,128)(2,1)S(1)}, bf16[128,2048]{1,0:T(8,128)(2,1)S(1)}, u32[]{:S(2)}, u32[]{:S(2)}) collective-permute-start(bf16[128,2048]{1,0:T(8,128)(2,1)S(1)} %collective-permute-done.27.refs_2_), channel_id=1, source_target_pairs={{0,1},{1,0},{2,3},{3,2},{4,5},{5,4},{6,7},{7,6},{8,9},{9,8},{10,11... | collective-permute-start | bytes 1572872 | tf_op jit(solution)/shard_map/ppermute | solution.py:494
  81.0 14.3 %collective-permute-start.34 = (bf16[128,2048]{1,0:T(8,128)(2,1)S(1)}, bf16[128,2048]{1,0:T(8,128)(2,1)S(1)}, u32[]{:S(2)}, u32[]{:S(2)}) collective-permute-start(bf16[128,2048]{1,0:T(8,128)(2,1)S(1)} %weave.3.refs_0_.refs_1_), channel_id=1, source_target_pairs={{0,16},{1,17},{2,18},{3,19},{4,20},{5,21},{6,22},{7,23},{8,24},{9,... | collective-permute-start | bytes 1572872 | tf_op jit(solution)/shard_map/ppermute | solution.py:502
  81.5 13.6 %collective-permute-start.30 = (bf16[128,2048]{1,0:T(8,128)(2,1)S(1)}, bf16[128,2048]{1,0:T(8,128)(2,1)S(1)}, u32[]{:S(2)}, u32[]{:S(2)}) collective-permute-start(bf16[128,2048]{1,0:T(8,128)(2,1)S(1)} %collective-permute-done.26.refs_0_), channel_id=1, source_target_pairs={{0,4},{1,5},{4,8},{5,9},{8,12},{9,13},{12,14},{13,15},{14,10},{15,... | collective-permute-start | bytes 1572872 | tf_op jit(solution)/shard_map/ppermute | solution.py:488
  81.9 13.3 %collective-permute-start.31 = (bf16[128,2048]{1,0:T(8,128)(2,1)S(1)}, bf16[128,2048]{1,0:T(8,128)(2,1)S(1)}, u32[]{:S(2)}, u32[]{:S(2)}) collective-permute-start(bf16[128,2048]{1,0:T(8,128)(2,1)S(1)} %collective-permute-done.27.refs_2_), channel_id=1, source_target_pairs={{4,0},{5,1},{8,4},{9,5},{12,8},{13,9},{14,12},{15,13},{10,14},{11,... | collective-permute-start | bytes 1572872 | tf_op jit(solution)/shard_map/ppermute | solution.py:491
  95.2 2.6 %collective-permute-start.37 = (bf16[128,2048]{1,0:T(8,128)(2,1)S(1)}, bf16[128,2048]{1,0:T(8,128)(2,1)S(1)}, u32[]{:S(2)}, u32[]{:S(2)}) collective-permute-start(bf16[128,2048]{1,0:T(8,128)(2,1)S(1)} %collective-permute-done.30.refs_0_), channel_id=1, source_target_pairs={{0,1},{1,0},{2,3},{3,2},{4,5},{5,4},{6,7},{7,6},{8,9},{9,8},{10,11... | collective-permute-start | bytes 1572872 | tf_op jit(solution)/shard_map/ppermute | solution.py:494
  95.2 2.7 %collective-permute-start.38 = (bf16[128,2048]{1,0:T(8,128)(2,1)S(1)}, bf16[128,2048]{1,0:T(8,128)(2,1)S(1)}, u32[]{:S(2)}, u32[]{:S(2)}) collective-permute-start(bf16[128,2048]{1,0:T(8,128)(2,1)S(1)} %collective-permute-done.31.refs_2_), channel_id=1, source_target_pairs={{0,1},{1,0},{2,3},{3,2},{4,5},{5,4},{6,7},{7,6},{8,9},{9,8},{10,11... | collective-permute-start | bytes 1572872 | tf_op jit(solution)/shard_map/ppermute | solution.py:494
  95.8 9.3 %collective-permute-start.36 = (bf16[64,2048]{1,0:T(8,128)(2,1)S(1)}, bf16[64,2048]{1,0:T(8,128)(2,1)S(1)}, u32[]{:S(2)}, u32[]{:S(2)}) collective-permute-start(bf16[64,2048]{1,0:T(8,128)(2,1)S(1)} %slice.7), channel_id=1, source_target_pairs={{4,0},{5,1},{8,4},{9,5},{12,8},{13,9},{14,12},{15,13},{10,14},{11,... | collective-permute-start | bytes 786440 | tf_op jit(solution)/shard_map/ppermute | solution.py:491
  97.4 7.9 %collective-permute-start.35 = (bf16[64,2048]{1,0:T(8,128)(2,1)S(1)}, bf16[64,2048]{1,0:T(8,128)(2,1)S(1)}, u32[]{:S(2)}, u32[]{:S(2)}) collective-permute-start(bf16[64,2048]{1,0:T(8,128)(2,1)S(1)} %slice.6), channel_id=1, source_target_pairs={{0,4},{1,5},{4,8},{5,9},{8,12},{9,13},{12,14},{13,15},{14,10},{15,... | collective-permute-start | bytes 786440 | tf_op jit(solution)/shard_map/ppermute | solution.py:488
  105.3 2.7 %collective-permute-start.39 = (bf16[256,2048]{1,0:T(8,128)(2,1)S(1)}, bf16[256,2048]{1,0:T(8,128)(2,1)S(1)}, u32[]{:S(2)}, u32[]{:S(2)}) collective-permute-start(bf16[256,2048]{1,0:T(8,128)(2,1)S(1)} %get-tuple-element.144), channel_id=1, source_target_pairs={{0,1},{1,0},{2,3},{3,2},{4,5},{5,4},{6,7},{7,6},{8,9},{9,8},{10,11... | collective-permute-start | bytes 3145736 | tf_op jit(solution)/shard_map/ppermute | solution.py:494
  105.3 4.9 %collective-permute-start.40 = (bf16[64,2048]{1,0:T(8,128)(2,1)S(1)}, bf16[64,2048]{1,0:T(8,128)(2,1)S(1)}, u32[]{:S(2)}, u32[]{:S(2)}) collective-permute-start(bf16[64,2048]{1,0:T(8,128)(2,1)S(1)} %collective-permute-done.35.refs_0_), channel_id=1, source_target_pairs={{0,1},{1,0},{2,3},{3,2},{4,5},{5,4},{6,7},{7,6},{8,9},{9,8},{10,11... | collective-permute-start | bytes 786440 | tf_op jit(solution)/shard_map/ppermute | solution.py:494
  105.9 4.4 %collective-permute-start.41 = (bf16[64,2048]{1,0:T(8,128)(2,1)S(1)}, bf16[64,2048]{1,0:T(8,128)(2,1)S(1)}, u32[]{:S(2)}, u32[]{:S(2)}) collective-permute-start(bf16[64,2048]{1,0:T(8,128)(2,1)S(1)} %collective-permute-done.36.refs_1_), channel_id=1, source_target_pairs={{0,1},{1,0},{2,3},{3,2},{4,5},{5,4},{6,7},{7,6},{8,9},{9,8},{10,11... | collective-permute-start | bytes 786440 | tf_op jit(solution)/shard_map/ppermute | solution.py:494
  105.9 16.2 %collective-permute-start.50 = (bf16[256,2048]{1,0:T(8,128)(2,1)S(1)}, bf16[256,2048]{1,0:T(8,128)(2,1)S(1)}, u32[]{:S(2)}, u32[]{:S(2)}) collective-permute-start(bf16[256,2048]{1,0:T(8,128)(2,1)S(1)} %get-tuple-element.167), channel_id=1, source_target_pairs={{0,1},{1,0},{2,3},{3,2},{4,5},{5,4},{6,7},{7,6},{8,9},{9,8},{10,11... | collective-permute-start | bytes 3145736 | tf_op jit(solution)/shard_map/ppermute | solution.py:494
  108.1 8.4 %collective-permute-start.42 = (bf16[64,2048]{1,0:T(8,128)(2,1)S(1)}, bf16[64,2048]{1,0:T(8,128)(2,1)S(1)}, u32[]{:S(2)}, u32[]{:S(2)}) collective-permute-start(bf16[64,2048]{1,0:T(8,128)(2,1)S(1)} %add.23), channel_id=1, source_target_pairs={{4,0},{5,1},{8,4},{9,5},{12,8},{13,9},{14,12},{15,13},{10,14},{11,... | collective-permute-start | bytes 786440 | tf_op jit(solution)/shard_map/ppermute | solution.py:491
  109.8 8.1 %collective-permute-start.43 = (bf16[64,2048]{1,0:T(8,128)(2,1)S(1)}, bf16[64,2048]{1,0:T(8,128)(2,1)S(1)}, u32[]{:S(2)}, u32[]{:S(2)}) collective-permute-start(bf16[64,2048]{1,0:T(8,128)(2,1)S(1)} %add.24), channel_id=1, source_target_pairs={{0,4},{1,5},{4,8},{5,9},{8,12},{9,13},{12,14},{13,15},{14,10},{15,... | collective-permute-start | bytes 786440 | tf_op jit(solution)/shard_map/ppermute | solution.py:488
  117.9 1.9 %collective-permute-start.44 = (bf16[128,2048]{1,0:T(8,128)(2,1)S(1)}, bf16[128,2048]{1,0:T(8,128)(2,1)S(1)}, u32[]{:S(2)}, u32[]{:S(2)}) collective-permute-start(bf16[128,2048]{1,0:T(8,128)(2,1)S(1)} %get-tuple-element.155), channel_id=1, source_target_pairs={{0,1},{1,0},{2,3},{3,2},{4,5},{5,4},{6,7},{7,6},{8,9},{9,8},{10,11... | collective-permute-start | bytes 1572872 | tf_op jit(solution)/shard_map/ppermute | solution.py:494
  117.9 22.1 %collective-permute-start.49 = (bf16[256,2048]{1,0:T(8,128)(2,1)S(1)}, bf16[256,2048]{1,0:T(8,128)(2,1)S(1)}, u32[]{:S(2)}, u32[]{:S(2)}) collective-permute-start(bf16[256,2048]{1,0:T(8,128)(2,1)S(1)} %get-tuple-element.165), channel_id=1, source_target_pairs={{0,1},{1,0},{2,3},{3,2},{4,5},{5,4},{6,7},{7,6},{8,9},{9,8},{10,11... | collective-permute-start | bytes 3145736 | tf_op jit(solution)/shard_map/ppermute | solution.py:494
  119.9 9.2 %collective-permute-start.45 = (bf16[64,2048]{1,0:T(8,128)(2,1)S(1)}, bf16[64,2048]{1,0:T(8,128)(2,1)S(1)}, u32[]{:S(2)}, u32[]{:S(2)}) collective-permute-start(bf16[64,2048]{1,0:T(8,128)(2,1)S(1)} %add.25), channel_id=1, source_target_pairs={{4,0},{5,1},{8,4},{9,5},{12,8},{13,9},{14,12},{15,13},{10,14},{11,... | collective-permute-start | bytes 786440 | tf_op jit(solution)/shard_map/ppermute | solution.py:491
  121.5 9.2 %collective-permute-start.55 = (bf16[64,2048]{1,0:T(8,128)(2,1)S(1)}, bf16[64,2048]{1,0:T(8,128)(2,1)S(1)}, u32[]{:S(2)}, u32[]{:S(2)}) collective-permute-start(bf16[64,2048]{1,0:T(8,128)(2,1)S(1)} %add.31), channel_id=1, source_target_pairs={{0,4},{1,5},{4,8},{5,9},{8,12},{9,13},{12,14},{13,15},{14,10},{15,... | collective-permute-start | bytes 786440 | tf_op jit(solution)/shard_map/ppermute | solution.py:488
  122.1 29.3 %collective-permute-start.47 = (bf16[128,2048]{1,0:T(8,128)(2,1)S(1)}, bf16[128,2048]{1,0:T(8,128)(2,1)S(1)}, u32[]{:S(2)}, u32[]{:S(2)}) collective-permute-start(bf16[128,2048]{1,0:T(8,128)(2,1)S(1)} %get-tuple-element.162), channel_id=1, source_target_pairs={{0,1},{1,0},{2,3},{3,2},{4,5},{5,4},{6,7},{7,6},{8,9},{9,8},{10,11... | collective-permute-start | bytes 1572872 | tf_op jit(solution)/shard_map/ppermute | solution.py:494
  122.2 19.4 %collective-permute-start.51 = (bf16[64,2048]{1,0:T(8,128)(2,1)S(1)}, bf16[64,2048]{1,0:T(8,128)(2,1)S(1)}, u32[]{:S(2)}, u32[]{:S(2)}) collective-permute-start(bf16[64,2048]{1,0:T(8,128)(2,1)S(1)} %add.27), channel_id=1, source_target_pairs={{4,0},{5,1},{8,4},{9,5},{12,8},{13,9},{14,12},{15,13},{10,14},{11,... | collective-permute-start | bytes 786440 | tf_op jit(solution)/shard_map/ppermute | solution.py:491
  129.2 10.3 %collective-permute-start.46 = (bf16[64,2048]{1,0:T(8,128)(2,1)S(1)}, bf16[64,2048]{1,0:T(8,128)(2,1)S(1)}, u32[]{:S(2)}, u32[]{:S(2)}) collective-permute-start(bf16[64,2048]{1,0:T(8,128)(2,1)S(1)} %add.26), channel_id=1, source_target_pairs={{4,0},{5,1},{8,4},{9,5},{12,8},{13,9},{14,12},{15,13},{10,14},{11,... | collective-permute-start | bytes 786440 | tf_op jit(solution)/shard_map/ppermute | solution.py:491
  130.9 6.8 %collective-permute-start.56 = (bf16[64,2048]{1,0:T(8,128)(2,1)S(1)}, bf16[64,2048]{1,0:T(8,128)(2,1)S(1)}, u32[]{:S(2)}, u32[]{:S(2)}) collective-permute-start(bf16[64,2048]{1,0:T(8,128)(2,1)S(1)} %add.32), channel_id=1, source_target_pairs={{0,4},{1,5},{4,8},{5,9},{8,12},{9,13},{12,14},{13,15},{14,10},{15,... | collective-permute-start | bytes 786440 | tf_op jit(solution)/shard_map/ppermute | solution.py:488
  137.7 9.0 %collective-permute-start.59 = (bf16[64,2048]{1,0:T(8,128)(2,1)S(1)}, bf16[64,2048]{1,0:T(8,128)(2,1)S(1)}, u32[]{:S(2)}, u32[]{:S(2)}) collective-permute-start(bf16[64,2048]{1,0:T(8,128)(2,1)S(1)} %add.35), channel_id=1, source_target_pairs={{0,4},{1,5},{4,8},{5,9},{8,12},{9,13},{12,14},{13,15},{14,10},{15,... | collective-permute-start | bytes 786440 | tf_op jit(solution)/shard_map/ppermute | solution.py:488
  139.5 10.1 %collective-permute-start.57 = (bf16[64,2048]{1,0:T(8,128)(2,1)S(1)}, bf16[64,2048]{1,0:T(8,128)(2,1)S(1)}, u32[]{:S(2)}, u32[]{:S(2)}) collective-permute-start(bf16[64,2048]{1,0:T(8,128)(2,1)S(1)} %add.33), channel_id=1, source_target_pairs={{0,4},{1,5},{4,8},{5,9},{8,12},{9,13},{12,14},{13,15},{14,10},{15,... | collective-permute-start | bytes 786440 | tf_op jit(solution)/shard_map/ppermute | solution.py:488
  139.9 13.1 %collective-permute-start.48 = (bf16[128,2048]{1,0:T(8,128)(2,1)S(1)}, bf16[128,2048]{1,0:T(8,128)(2,1)S(1)}, u32[]{:S(2)}, u32[]{:S(2)}) collective-permute-start(bf16[128,2048]{1,0:T(8,128)(2,1)S(1)} %get-tuple-element.163), channel_id=1, source_target_pairs={{0,16},{1,17},{2,18},{3,19},{4,20},{5,21},{6,22},{7,23},{8,24},{9,... | collective-permute-start | bytes 1572872 | tf_op jit(solution)/shard_map/ppermute | solution.py:502
  141.5 9.3 %collective-permute-start.53 = (bf16[64,2048]{1,0:T(8,128)(2,1)S(1)}, bf16[64,2048]{1,0:T(8,128)(2,1)S(1)}, u32[]{:S(2)}, u32[]{:S(2)}) collective-permute-start(bf16[64,2048]{1,0:T(8,128)(2,1)S(1)} %add.29), channel_id=1, source_target_pairs={{4,0},{5,1},{8,4},{9,5},{12,8},{13,9},{14,12},{15,13},{10,14},{11,... | collective-permute-start | bytes 786440 | tf_op jit(solution)/shard_map/ppermute | solution.py:491
  146.6 9.8 %collective-permute-start.52 = (bf16[64,2048]{1,0:T(8,128)(2,1)S(1)}, bf16[64,2048]{1,0:T(8,128)(2,1)S(1)}, u32[]{:S(2)}, u32[]{:S(2)}) collective-permute-start(bf16[64,2048]{1,0:T(8,128)(2,1)S(1)} %add.28), channel_id=1, source_target_pairs={{4,0},{5,1},{8,4},{9,5},{12,8},{13,9},{14,12},{15,13},{10,14},{11,... | collective-permute-start | bytes 786440 | tf_op jit(solution)/shard_map/ppermute | solution.py:491
  149.6 8.5 %collective-permute-start.60 = (bf16[64,2048]{1,0:T(8,128)(2,1)S(1)}, bf16[64,2048]{1,0:T(8,128)(2,1)S(1)}, u32[]{:S(2)}, u32[]{:S(2)}) collective-permute-start(bf16[64,2048]{1,0:T(8,128)(2,1)S(1)} %add.36), channel_id=1, source_target_pairs={{0,4},{1,5},{4,8},{5,9},{8,12},{9,13},{12,14},{13,15},{14,10},{15,... | collective-permute-start | bytes 786440 | tf_op jit(solution)/shard_map/ppermute | solution.py:488
  150.8 10.1 %collective-permute-start.58 = (bf16[64,2048]{1,0:T(8,128)(2,1)S(1)}, bf16[64,2048]{1,0:T(8,128)(2,1)S(1)}, u32[]{:S(2)}, u32[]{:S(2)}) collective-permute-start(bf16[64,2048]{1,0:T(8,128)(2,1)S(1)} %add.34), channel_id=1, source_target_pairs={{0,4},{1,5},{4,8},{5,9},{8,12},{9,13},{12,14},{13,15},{14,10},{15,... | collective-permute-start | bytes 786440 | tf_op jit(solution)/shard_map/ppermute | solution.py:488
  151.4 9.6 %collective-permute-start.54 = (bf16[64,2048]{1,0:T(8,128)(2,1)S(1)}, bf16[64,2048]{1,0:T(8,128)(2,1)S(1)}, u32[]{:S(2)}, u32[]{:S(2)}) collective-permute-start(bf16[64,2048]{1,0:T(8,128)(2,1)S(1)} %add.30), channel_id=1, source_target_pairs={{4,0},{5,1},{8,4},{9,5},{12,8},{13,9},{14,12},{15,13},{10,14},{11,... | collective-permute-start | bytes 786440 | tf_op jit(solution)/shard_map/ppermute | solution.py:491
  (4 other events, 68.1 us)
